TPU v7x, 32 devices: a whole 2x2x4 slice. The times are simulated.
32 devices in a mesh: dp: 16 (over z, x, core), seq: 2 (over y).
Axes of the slice: x: 2, y: 2, z: 4, core: 2. Of those that a mesh axis runs over, the one named last changes fastest.
Arguments:
- tokens: bfloat16 [8192, 1024], P(('dp', 'seq')), may hold values from -6 to 6
- memory: bfloat16 [8192, 1024], P(('dp', 'seq')), may hold values from -6 to 6
- attn_bank: bfloat16 [8192, 1024], P(('dp', 'seq')), may hold values from -2.828427 to 2.828427
- ffn_bank: bfloat16 [8192, 1024], P(('dp', 'seq')), may hold values from -0.375 to 0.375
- norm_params: float32 [6, 1024], replicated, may hold values from 0.1 to 1.9
- prefix: int32 [16], P('dp'), may hold values from 0 to 256, as said below
- cotangent: bfloat16 [8192, 1024], P(('dp', 'seq')), may hold values from -6 to 6
Outputs:
- output: float32 [8192, 1024], P(('dp', 'seq'))
- d_tokens: float32 [8192, 1024], P(('dp', 'seq'))
- d_memory: float32 [8192, 1024], P(('dp', 'seq'))
- d_attn_bank: float32 [8192, 1024], P(('dp', 'seq'))
- d_ffn_bank: float32 [8192, 1024], P(('dp', 'seq'))
- d_norm_params: float32 [6, 1024], replicated
Inputs may be any that keep to these rules, and one draw needn't show every extreme that they name: `prefix`: 0 in some pair and 256 in another.
All inputs are finite; a program needn't handle non-finite values.
Results may differ from a plain program's by a relative error of at most 0.025.
Values may be sent and summed in bfloat16 or wider, within the bound.
A program may use at most 192 MiB of HBM per device.

v0:
```python
import jax
import jax.numpy as jnp
from jax import lax
from jax.sharding import PartitionSpec as P

HD = 64


alpha_scale = 300.0**0.25
norm_eps = 1e-05
masked_score = -1e30


def matmul(left, right):
    return jnp.dot(left, right, preferred_element_type=jnp.float32)


def matmul_nt(left, right):
    return lax.dot_general(
        left, right, (((1,), (1,)), ((), ())), preferred_element_type=jnp.float32
    )


def matmul_tn(left, right):
    return lax.dot_general(
        left, right, (((0,), (0,)), ((), ())), preferred_element_type=jnp.float32
    )


def norm_forward(summed, gain_row, shift_row):
    centred = summed - jnp.mean(summed, axis=-1, keepdims=True)
    inv_std = lax.rsqrt(jnp.mean(centred * centred, axis=-1, keepdims=True) + norm_eps)
    normed = centred * inv_std
    return (normed * gain_row + shift_row, normed, inv_std)


def norm_backward(gradient, normed, inv_std, gain_row):
    scaled_grad = gradient * gain_row
    plain_mean = jnp.mean(scaled_grad, axis=-1, keepdims=True)
    normed_mean = jnp.mean(scaled_grad * normed, axis=-1, keepdims=True)
    summed_grad = inv_std * (scaled_grad - plain_mean - normed * normed_mean)
    return (summed_grad, jnp.sum(gradient * normed, axis=0), jnp.sum(gradient, axis=0))


def attend(queries, key_rows, value_rows, visible, head_dim):
    row_count, model_width = queries.shape
    group_width = 2 * head_dim
    score_scale = head_dim ** (-0.5)

    def one_group(running, group_index):
        column = group_index * group_width
        query_part = lax.dynamic_slice_in_dim(queries, column, group_width, 1).reshape(
            row_count, 2, head_dim
        )
        key_part = lax.dynamic_slice_in_dim(key_rows, column, group_width, 1).reshape(
            -1, 2, head_dim
        )
        value_part = lax.dynamic_slice_in_dim(value_rows, column, group_width, 1).reshape(
            -1, 2, head_dim
        )
        scores = (
            jnp.einsum("qhd,khd->hqk", query_part, key_part, preferred_element_type=jnp.float32)
            * score_scale
        )
        if visible is not None:
            scores = jnp.where(visible[None], scores, masked_score)
        highest = jnp.max(scores, axis=-1, keepdims=True)
        exponent = jnp.exp(scores - highest)
        totals = jnp.sum(exponent, axis=-1, keepdims=True)
        weights = (exponent / totals).astype(jnp.bfloat16)
        mixed_rows = jnp.einsum(
            "hqk,khd->qhd", weights, value_part, preferred_element_type=jnp.float32
        )
        running = lax.dynamic_update_slice_in_dim(
            running, mixed_rows.reshape(row_count, group_width), column, 1
        )
        return (running, (highest + jnp.log(totals))[..., 0])

    initial = jnp.zeros((row_count, model_width), jnp.float32)
    outputs, log_sums = lax.scan(one_group, initial, jnp.arange(model_width // group_width))
    return (outputs.astype(jnp.bfloat16), log_sums)


def attend_back(queries, key_rows, value_rows, visible, head_dim, out_grad, log_sums):
    row_count, model_width = queries.shape
    key_count = key_rows.shape[0]
    group_width = 2 * head_dim
    score_scale = head_dim ** (-0.5)

    def one_group(running, group_items):
        group_index, group_sums = group_items
        query_acc, key_acc, value_acc = running
        column = group_index * group_width
        query_part = lax.dynamic_slice_in_dim(queries, column, group_width, 1).reshape(
            row_count, 2, head_dim
        )
        key_part = lax.dynamic_slice_in_dim(key_rows, column, group_width, 1).reshape(
            key_count, 2, head_dim
        )
        value_part = lax.dynamic_slice_in_dim(value_rows, column, group_width, 1).reshape(
            key_count, 2, head_dim
        )
        grad_part = lax.dynamic_slice_in_dim(out_grad, column, group_width, 1).reshape(
            row_count, 2, head_dim
        )
        scores = (
            jnp.einsum("qhd,khd->hqk", query_part, key_part, preferred_element_type=jnp.float32)
            * score_scale
        )
        if visible is not None:
            scores = jnp.where(visible[None], scores, masked_score)
        probs = jnp.exp(scores - group_sums[..., None])
        prob_grad = jnp.einsum(
            "qhd,khd->hqk", grad_part, value_part, preferred_element_type=jnp.float32
        )
        row_dot = jnp.sum(prob_grad * probs, axis=-1, keepdims=True)
        score_grad = (probs * (prob_grad - row_dot)).astype(jnp.bfloat16)
        query_piece = (
            jnp.einsum("hqk,khd->qhd", score_grad, key_part, preferred_element_type=jnp.float32)
            * score_scale
        )
        key_piece = (
            jnp.einsum("hqk,qhd->khd", score_grad, query_part, preferred_element_type=jnp.float32)
            * score_scale
        )
        value_piece = jnp.einsum(
            "hqk,qhd->khd",
            probs.astype(jnp.bfloat16),
            grad_part,
            preferred_element_type=jnp.float32,
        )
        query_acc = lax.dynamic_update_slice_in_dim(
            query_acc, query_piece.reshape(row_count, group_width), column, 1
        )
        key_acc = lax.dynamic_update_slice_in_dim(
            key_acc, key_piece.reshape(key_count, group_width), column, 1
        )
        value_acc = lax.dynamic_update_slice_in_dim(
            value_acc, value_piece.reshape(key_count, group_width), column, 1
        )
        return ((query_acc, key_acc, value_acc), None)

    initial = (
        jnp.zeros((row_count, model_width), jnp.float32),
        jnp.zeros((key_count, model_width), jnp.float32),
        jnp.zeros((key_count, model_width), jnp.float32),
    )
    results, unused = lax.scan(
        one_group, initial, (jnp.arange(model_width // group_width), log_sums)
    )
    return results


def on_device(tokens, memory, attn_bank, ffn_bank, norm_params, prefix, cotangent):
    row_count, model_width = tokens.shape
    head_dim = HD
    attn_full, ffn_full = (
        lax.all_gather(attn_bank, ("dp", "seq"), axis=0, tiled=True),
        lax.all_gather(ffn_bank, ("dp", "seq"), axis=0, tiled=True),
    )
    blocks = attn_full.reshape(8, model_width, model_width)
    hidden_units = ffn_full.shape[0] // 2
    weight_in = ffn_full[:hidden_units]
    weight_out = ffn_full[hidden_units:]
    key_self = matmul(tokens, blocks[1]).astype(jnp.bfloat16)
    value_self = matmul(tokens, blocks[2]).astype(jnp.bfloat16)
    key_cross = matmul(memory, blocks[5]).astype(jnp.bfloat16)
    value_cross = matmul(memory, blocks[6]).astype(jnp.bfloat16)
    all_key_self, all_value_self, all_key_cross, all_value_cross = (
        lax.all_gather(key_self, "seq", axis=0, tiled=True),
        lax.all_gather(value_self, "seq", axis=0, tiled=True),
        lax.all_gather(key_cross, "seq", axis=0, tiled=True),
        lax.all_gather(value_cross, "seq", axis=0, tiled=True),
    )
    query_self = matmul(tokens, blocks[0]).astype(jnp.bfloat16)
    seq_length = all_key_self.shape[0]
    row_start = lax.axis_index("seq") * row_count
    query_pos = row_start + jnp.arange(row_count, dtype=jnp.int32)
    key_pos = jnp.arange(seq_length, dtype=jnp.int32)
    visible = (key_pos[None, :] <= query_pos[:, None]) | (key_pos[None, :] < prefix[0])
    mixed_self, sums_self = attend(query_self, all_key_self, all_value_self, visible, head_dim)
    first_sum = alpha_scale * tokens.astype(jnp.float32) + matmul(mixed_self, blocks[3])
    first_out, first_normed, first_inv = norm_forward(first_sum, norm_params[0], norm_params[3])
    first_low = first_out.astype(jnp.bfloat16)
    query_cross = matmul(first_low, blocks[4]).astype(jnp.bfloat16)
    mixed_cross, sums_cross = attend(query_cross, all_key_cross, all_value_cross, None, head_dim)
    second_sum = alpha_scale * first_out + matmul(mixed_cross, blocks[7])
    second_out, second_normed, second_inv = norm_forward(second_sum, norm_params[1], norm_params[4])
    second_low = second_out.astype(jnp.bfloat16)
    hidden_pre = matmul_nt(second_low, weight_in)
    hidden_act = jax.nn.silu(hidden_pre).astype(jnp.bfloat16)
    third_sum = alpha_scale * second_out + matmul(hidden_act, weight_out)
    output, third_normed, third_inv = norm_forward(third_sum, norm_params[2], norm_params[5])
    attn_back, ffn_back = (
        lax.all_gather(attn_bank, ("dp", "seq"), axis=0, tiled=True),
        lax.all_gather(ffn_bank, ("dp", "seq"), axis=0, tiled=True),
    )
    back_blocks = attn_back.reshape(8, model_width, model_width)
    back_in = ffn_back[:hidden_units]
    back_out = ffn_back[hidden_units:]
    third_grad, gain_three, shift_three = norm_backward(
        cotangent.astype(jnp.float32), third_normed, third_inv, norm_params[2]
    )
    ffn_out_grad = third_grad.astype(jnp.bfloat16)
    grad_weight_out = matmul_tn(hidden_act, ffn_out_grad)
    act_grad = matmul_nt(ffn_out_grad, back_out)
    sigmoid_pre = jax.nn.sigmoid(hidden_pre)
    slope = sigmoid_pre * (1.0 + hidden_pre * (1.0 - sigmoid_pre))
    pre_grad = (act_grad * slope).astype(jnp.bfloat16)
    grad_weight_in = matmul_tn(pre_grad, second_low)
    ffn_terms = jnp.concatenate([grad_weight_in, grad_weight_out], axis=0)
    second_in = alpha_scale * third_grad + matmul(pre_grad, back_in)
    second_grad, gain_two, shift_two = norm_backward(
        second_in, second_normed, second_inv, norm_params[1]
    )
    cross_branch_grad = second_grad.astype(jnp.bfloat16)
    grad_out_cross = matmul_tn(mixed_cross, cross_branch_grad)
    cross_mixed_grad = matmul_nt(cross_branch_grad, back_blocks[7]).astype(jnp.bfloat16)
    cross_query_grad, cross_key_part, cross_value_part = attend_back(
        query_cross, all_key_cross, all_value_cross, None, head_dim, cross_mixed_grad, sums_cross
    )
    key_cross_grad, value_cross_grad = (
        lax.psum_scatter(
            cross_key_part.astype(jnp.bfloat16), "seq", scatter_dimension=0, tiled=True
        ).astype(jnp.float32),
        lax.psum_scatter(
            cross_value_part.astype(jnp.bfloat16), "seq", scatter_dimension=0, tiled=True
        ).astype(jnp.float32),
    )
    cross_query_low = cross_query_grad.astype(jnp.bfloat16)
    key_cross_low = key_cross_grad.astype(jnp.bfloat16)
    value_cross_low = value_cross_grad.astype(jnp.bfloat16)
    grad_query_cross = matmul_tn(first_low, cross_query_low)
    grad_key_cross = matmul_tn(memory, key_cross_low)
    grad_value_cross = matmul_tn(memory, value_cross_low)
    memory_grad = matmul_nt(key_cross_low, back_blocks[5]) + matmul_nt(
        value_cross_low, back_blocks[6]
    )
    first_in = alpha_scale * second_grad + matmul_nt(cross_query_low, back_blocks[4])
    first_grad, gain_one, shift_one = norm_backward(
        first_in, first_normed, first_inv, norm_params[0]
    )
    self_branch_grad = first_grad.astype(jnp.bfloat16)
    grad_out_self = matmul_tn(mixed_self, self_branch_grad)
    self_mixed_grad = matmul_nt(self_branch_grad, back_blocks[3]).astype(jnp.bfloat16)
    self_query_grad, self_key_part, self_value_part = attend_back(
        query_self, all_key_self, all_value_self, visible, head_dim, self_mixed_grad, sums_self
    )
    key_self_grad, value_self_grad = (
        lax.psum_scatter(
            self_key_part.astype(jnp.bfloat16), "seq", scatter_dimension=0, tiled=True
        ).astype(jnp.float32),
        lax.psum_scatter(
            self_value_part.astype(jnp.bfloat16), "seq", scatter_dimension=0, tiled=True
        ).astype(jnp.float32),
    )
    self_query_low = self_query_grad.astype(jnp.bfloat16)
    key_self_low = key_self_grad.astype(jnp.bfloat16)
    value_self_low = value_self_grad.astype(jnp.bfloat16)
    grad_query_self = matmul_tn(tokens, self_query_low)
    grad_key_self = matmul_tn(tokens, key_self_low)
    grad_value_self = matmul_tn(tokens, value_self_low)
    token_grad = (
        alpha_scale * first_grad
        + matmul_nt(self_query_low, back_blocks[0])
        + matmul_nt(key_self_low, back_blocks[1])
        + matmul_nt(value_self_low, back_blocks[2])
    )
    attn_terms = jnp.concatenate(
        [
            grad_query_self,
            grad_key_self,
            grad_value_self,
            grad_out_self,
            grad_query_cross,
            grad_key_cross,
            grad_value_cross,
            grad_out_cross,
        ],
        axis=0,
    )
    attn_shard, ffn_shard = (
        lax.psum_scatter(attn_terms, ("dp", "seq"), scatter_dimension=0, tiled=True),
        lax.psum_scatter(ffn_terms, ("dp", "seq"), scatter_dimension=0, tiled=True),
    )
    norm_terms = jnp.stack([gain_one, gain_two, gain_three, shift_one, shift_two, shift_three])
    norm_grad = lax.psum(norm_terms, ("dp", "seq"))
    return (output, token_grad, memory_grad, attn_shard, ffn_shard, norm_grad)


def solution(mesh):
    return jax.shard_map(
        on_device,
        mesh=mesh,
        in_specs=(
            P(("dp", "seq"), None),
            P(("dp", "seq"), None),
            P(("dp", "seq"), None),
            P(("dp", "seq"), None),
            P(),
            P("dp"),
            P(("dp", "seq"), None),
        ),
        out_specs=(
            P(("dp", "seq"), None),
            P(("dp", "seq"), None),
            P(("dp", "seq"), None),
            P(("dp", "seq"), None),
            P(("dp", "seq"), None),
            P(),
        ),
        check_vma=False,
    )
```

profile of v0, /device:TPU:0, one launch (start us, length us, event | category | flops | bytes accessed | tf_op | source)
XLA Modules:
  0.0 2029.2 jit_solution(10930400100170669816)
XLA Ops:
  8.0 120.5 %all-gather.7.cloned.1.call-done = bf16[8192,1024]{1,0:T(8,128)(2,1)} async-done(((bf16[256,1024]{1,0:T(8,128)(2,1)}), bf16[8192,1024]{1,0:T(8,128)(2,1)}) %all-gather.7.cloned.1.call-update) | async-done | bytes 16777232 | tf_op jit(solution)/shard_map/all_gather | solution.py:158
  128.5 3.3 fusion.102
  131.9 3.3 fusion.96
  135.3 3.2 fusion.114
  138.5 3.1 fusion.108
  143.0 2.3 fusion.99
  145.3 1.1 copy.14
  146.4 5.1 all-gather.11.cloned.1.call-done
  151.4 1.5 copy.15
  152.9 22.0 %all-gather.9.cloned.1.call-done = bf16[512,1024]{1,0:T(8,128)(2,1)} async-done(((bf16[256,1024]{1,0:T(8,128)(2,1)}), bf16[512,1024]{1,0:T(8,128)(2,1)}) %all-gather.9.cloned.1.call-update) | async-done | bytes 1048592 | tf_op jit(solution)/shard_map/all_gather | solution.py:171
  174.9 1.5 copy.13
  177.3 33.4 %while.56 = (s32[]{:T(128)}, bf16[256,1024]{0,1:T(8,128)(2,1)}, f32[8,2,256]{2,1,0:T(2,128)S(1)}, s32[8]{0:T(128)S(1)}, bf16[512,1024]{0,1:T(8,128)(2,1)S(1)}, /...) while((s32[]{:T(128)}, bf16[256,1024]{0,1:T(8,128)(2,1)}, ...), condition=%wide.region_3.4_spmd.clone, body=%wide.region_0.3_spmd.clone.sunk | while | flops 69467648 | bytes 4605647 | solution.py:80
  211.7 2.9 fusion.151
  214.9 3.1 fusion.111
  218.1 2.0 copy.17
  220.1 2.3 copy.18
  222.4 2.3 copy.16
  225.5 39.7 %while.54 = (s32[]{:T(128)}, bf16[256,1024]{0,1:T(8,128)(2,1)}, f32[8,2,256]{2,1,0:T(2,128)S(1)}, s32[8]{0:T(128)S(1)}, bf16[512,1024]{0,1:T(8,128)(2,1)}, /*ind...) while((s32[]{:T(128)}, bf16[256,1024]{0,1:T(8,128)(2,1)}, ...), condition=%wide.region_9.10_spmd, body=%wide.region_6.9_spmd.sunk | while | flops 68943360 | bytes 4341951 | solution.py:80
  227.6 1.0 constant_dynamic-slice_fusion.26
  232.5 1.0 constant_dynamic-slice_fusion.26
  237.5 1.0 constant_dynamic-slice_fusion.26
  242.4 1.0 constant_dynamic-slice_fusion.26
  247.4 1.0 constant_dynamic-slice_fusion.26
  252.3 1.0 constant_dynamic-slice_fusion.26
  257.2 1.0 constant_dynamic-slice_fusion.26
  262.2 1.0 constant_dynamic-slice_fusion.26
  265.2 2.6 fusion.152
  268.1 71.1 %all-gather.17.cloned.1.call-done = bf16[8192,1024]{1,0:T(8,128)(2,1)} async-done(((bf16[256,1024]{1,0:T(8,128)(2,1)}), bf16[8192,1024]{1,0:T(8,128)(2,1)}) %all-gather.17.cloned.1.call-update) | async-done | bytes 16777232 | tf_op jit(solution)/shard_map/all_gather | solution.py:159
  339.2 5.8 fusion.26
  345.1 7.6 fusion.153
  353.0 1.5 fusion.123
  354.4 6.5 fusion.31
  361.0 6.1 multiply_reduce_fusion.2
  368.4 3.2 fusion.117
  372.4 1.0 broadcast.162.clone.2
  373.5 1.1 broadcast.162.clone.1
  374.5 63.9 %while.55 = (s32[]{:T(128)}, bf16[256,1024]{0,1:T(8,128)(2,1)}, bf16[512,1024]{0,1:T(8,128)(2,1)}, bf16[512,1024]{0,1:T(8,128)(2,1)}, s32[8]{0:T(128)S(1)}, /*in...) while((s32[]{:T(128)}, bf16[256,1024]{0,1:T(8,128)(2,1)}, ...), condition=%wide.region_20.21_spmd, body=%wide.region_18.20_spmd.sunk | while | flops 170065408 | bytes 10430691 | solution.py:148
  438.4 3.1 multiply_reduce_fusion.3
  441.9 1.0 copy-done.1
  442.9 3.2 fusion.105
  446.9 1.0 broadcast.162.clone
  448.0 1.0 broadcast.162
  449.0 65.7 %while.57 = (s32[]{:T(128)}, bf16[256,1024]{0,1:T(8,128)(2,1)}, bf16[512,1024]{0,1:T(8,128)(2,1)}, bf16[512,1024]{0,1:T(8,128)(2,1)}, s32[8]{0:T(128)S(1)}, /*in...) while((s32[]{:T(128)}, bf16[256,1024]{0,1:T(8,128)(2,1)}, ...), condition=%wide.region_25.26_spmd.clone, body=%wide.region_23.25_spmd.clone.sunk | while | flops 170589696 | bytes 10694387 | solution.py:148
  516.3 11.2 fusion.134
  527.5 4.2 fusion.141
  531.7 18.9 pad_maximum_fusion
  551.7 2.8 bitcast_dynamic-update-slice_fusion.6
  554.5 3.8 bitcast_dynamic-update-slice_fusion.5
  558.4 3.8 bitcast_dynamic-update-slice_fusion.4
  562.2 2.7 convolution_dynamic-update-slice_fusion.2
  564.8 2.9 convolution_dynamic-update-slice_fusion.1
  567.8 11.5 reduce-scatter.11.cloned.1.call-done
  579.2 3.8 bitcast_dynamic-update-slice_fusion.3
  583.0 18.8 reduce-scatter.13.cloned.1.call-done
  601.8 3.7 bitcast_dynamic-update-slice_fusion.2
  605.5 2.6 convolution_dynamic-update-slice_fusion
  608.3 46.9 %psum.7 = f32[6,1024]{1,0:T(8,128)} all-reduce(f32[6,1024]{1,0:T(8,128)S(1)} %stack.27), channel_id=1, replica_groups=mesh['dp'=16,'seq'=2] {'dp','seq'}, use_global_device_ids=true, to_apply=%region_38.39 | all-reduce | flops 6144 | bytes 49152 | tf_op jit(solution)/shard_map/psum | solution.py:287
  655.2 2.6 fusion.38
  657.8 2.3 fusion.54
  660.1 3.3 fusion.81
  663.5 2.4 fusion.75
  665.9 3.4 fusion.69
  669.3 642.7 %reduce-scatter.17.cloned.1.call-done = f32[256,1024]{1,0:T(8,128)} async-done(((f32[8192,1024]{1,0:T(8,128)}), f32[256,1024]{1,0:T(8,128)}) %reduce-scatter.17.cloned.1.call-update) | async-done | bytes 1048592 | tf_op jit(solution)/shard_map/reduce_scatter | solution.py:284
  1312.0 709.8 %reduce-scatter.15.cloned.1.call-done = f32[256,1024]{1,0:T(8,128)} async-done(((f32[8192,1024]{1,0:T(8,128)}), f32[256,1024]{1,0:T(8,128)}) %reduce-scatter.15.cloned.1.call-update) | async-done | bytes 1048592 | tf_op jit(solution)/shard_map/reduce_scatter | solution.py:283
  (475 shorter events, 183.3 us)
Async XLA Ops:
  7.2 128.1 %copy-start = (bf16[256,1024]{1,0:T(8,128)(2,1)S(1)}, bf16[256,1024]{1,0:T(8,128)(2,1)}, u32[]{:S(2)}) copy-start(bf16[256,1024]{1,0:T(8,128)(2,1)} %param.16) | copy-start | bytes 1572868
  7.2 121.3 %all-gather.7.cloned.1.call-start = ((), (), s32[]{:S(2)}) async-start(), calls=%async_computation.6 | async-start | bytes 17301504 | tf_op jit(solution)/shard_map/all_gather | solution.py:158
  7.9 143.5 %all-gather.11.cloned.1.call-start = ((), (), s32[]{:S(2)}) async-start(), calls=%async_computation.8 | async-start | bytes 1572864 | tf_op jit(solution)/shard_map/all_gather | solution.py:170
  131.8 11.2 copy-start.19
  131.8 11.2 copy-start.3
  131.8 43.1 %all-gather.9.cloned.1.call-start = ((), (), s32[]{:S(2)}) async-start(), calls=%async_computation.7 | async-start | bytes 1572864 | tf_op jit(solution)/shard_map/all_gather | solution.py:171
  135.2 84.9 %all-gather.15.cloned.1.call-start = ((), (), s32[]{:S(2)}) async-start(), calls=%async_computation.10 | async-start | bytes 1572864 | tf_op jit(solution)/shard_map/all_gather | solution.py:172
  138.5 83.9 %all-gather.13.cloned.1.call-start = ((), (), s32[]{:S(2)}) async-start(), calls=%async_computation.9 | async-start | bytes 1572864 | tf_op jit(solution)/shard_map/all_gather | solution.py:173
  141.7 197.6 %all-gather.17.cloned.1.call-start = ((), (), s32[]{:S(2)}) async-start(), calls=%async_computation.11 | async-start | bytes 17301504 | tf_op jit(solution)/shard_map/all_gather | solution.py:159
  142.2 412.3 %reduce-scatter.7.cloned.1.call-start = ((), (), s32[]{:S(2)}) async-start(), calls=%async_computation.12 | async-start | bytes 1572864 | tf_op jit(solution)/shard_map/reduce_scatter | solution.py:250
  210.7 1.0 copy-start.6
  211.7 13.8 copy-start.7
  345.0 9.4 copy-start.20
  345.0 7.9 copy-start.18
  352.7 8.3 copy-start.9
  360.9 6.1 copy-start.14
  367.5 1.0 copy-start.10
  441.9 1.0 copy-start.1
  514.8 43.6 %reduce-scatter.9.cloned.1.call-start = ((), (), s32[]{:S(2)}) async-start(), calls=%async_computation.13 | async-start | bytes 1572864 | tf_op jit(solution)/shard_map/reduce_scatter | solution.py:253
  515.5 63.7 %reduce-scatter.11.cloned.1.call-start = ((), (), s32[]{:S(2)}) async-start(), calls=%async_computation.14 | async-start | bytes 1572864 | tf_op jit(solution)/shard_map/reduce_scatter | solution.py:223
  516.2 85.5 %reduce-scatter.13.cloned.1.call-start = ((), (), s32[]{:S(2)}) async-start(), calls=%async_computation.15 | async-start | bytes 1572864 | tf_op jit(solution)/shard_map/reduce_scatter | solution.py:226
  527.5 784.5 %reduce-scatter.17.cloned.1.call-start = ((), (), s32[]{:S(2)}) async-start(), calls=%async_computation.17 | async-start | bytes 34603008 | tf_op jit(solution)/shard_map/reduce_scatter | solution.py:284
  550.7 1.1 copy-start.4
  550.7 1471.2 %reduce-scatter.15.cloned.1.call-start = ((), (), s32[]{:S(2)}) async-start(), calls=%async_computation.16 | async-start | bytes 34603008 | tf_op jit(solution)/shard_map/reduce_scatter | solution.py:283
  554.5 7.6 copy-start.2
  558.4 3.8 copy-start.8
  558.4 6.5 copy-start.15
  567.7 37.8 %copy-start.11 = (f32[256,1024]{1,0:T(8,128)S(1)}, f32[256,1024]{1,0:T(8,128)}, u32[]{:S(2)}) copy-start(f32[256,1024]{1,0:T(8,128)} %copy-done.10) | copy-start | bytes 3145732
  567.7 37.8 %copy-start.16 = (bf16[256,1024]{0,1:T(8,128)(2,1)S(1)}, bf16[256,1024]{0,1:T(8,128)(2,1)}, u32[]{:S(2)}) copy-start(bf16[256,1024]{0,1:T(8,128)(2,1)} %get-tuple-element.201) | copy-start | bytes 1572868
  608.2 49.6 %copy-start.17 = (bf16[256,1024]{0,1:T(8,128)(2,1)S(1)}, bf16[256,1024]{0,1:T(8,128)(2,1)}, u32[]{:S(2)}) copy-start(bf16[256,1024]{0,1:T(8,128)(2,1)} %reduce-scatter.7.cloned.1.call-done) | copy-start | bytes 1572868
  608.2 51.9 %copy-start.13 = (bf16[256,1024]{0,1:T(8,128)(2,1)S(1)}, bf16[256,1024]{0,1:T(8,128)(2,1)}, u32[]{:S(2)}) copy-start(bf16[256,1024]{0,1:T(8,128)(2,1)} %reduce-scatter.13.cloned.1.call-done) | copy-start | bytes 1572868
  608.2 55.3 %copy-start.5 = (bf16[256,1024]{0,1:T(8,128)(2,1)S(1)}, bf16[256,1024]{0,1:T(8,128)(2,1)}, u32[]{:S(2)}) copy-start(bf16[256,1024]{0,1:T(8,128)(2,1)} %get-tuple-element.205) | copy-start | bytes 1572868
  655.2 10.7 copy-start.12
Sparse Core Ops, SparseCore 0:
  10.9 117.5 all-gather.6
  131.9 19.4 all-gather.10
  153.6 21.2 all-gather.8
  176.9 21.2 all-gather.14
  200.2 21.2 all-gather.12
  224.3 114.8 all-gather.16
  514.9 18.4 reduce-scatter.6
  536.3 20.3 reduce-scatter.8
  558.9 20.2 reduce-scatter.10
  581.4 20.3 reduce-scatter.12
  604.7 707.3 reduce-scatter.16
  1314.7 707.0 reduce-scatter.14
where the time goes:
time: 2040 us; the launch traced here: 2030 us
  waiting for transfers between devices  1600 us (78%)
  matrix products  154 us (8%)
  local copies, waits for them, and re-layouts  152 us (7%)
  blocking collectives  46.9 us (2%)
  other arithmetic  32.2 us (2%)
  loops' own time  22.6 us (1%)
    reduce_scatter x1, waiting for transfers between devices, on_device(): lax.psum_scatter(attn_terms, ('dp', 'seq'), scatter_dimension=0, tiled=True)  710 us
    reduce_scatter x1, waiting for transfers between devices, on_device(): lax.psum_scatter(ffn_terms, ('dp', 'seq'), scatter_dimension=0, tiled=True)  643 us
    all_gather x1, waiting for transfers between devices, on_device(): lax.all_gather(attn_bank, ('dp', 'seq'), axis=0, tiled=True)  121 us
    all_gather x1, waiting for transfers between devices, on_device(): lax.all_gather(ffn_bank, ('dp', 'seq'), axis=0, tiled=True)  71.1 us
    psum x1, blocking collectives, on_device(): norm_grad = lax.psum(norm_terms, ('dp', 'seq'))  46.9 us
    dot_general x10, matrix products, matmul_tn(): lax.dot_general(left, right, (((0,), (0,)), ((), ())), preferred_element_...  41.5 us
  transfers between devices with their start and end apart: 12, of which 8 were waited for; matrix products, arithmetic and copies ran while one was open for 8% of the time, Pallas kernels for 0%

commit v1 on v0

v1 whole, which is shorter than its diff:
```python
import functools

import jax
import jax.numpy as jnp
from jax import lax
from jax.experimental import pallas as pl
from jax.experimental.pallas import tpu as pltpu
from jax.sharding import PartitionSpec as P

HD = 64
PAIR = 2 * HD
TILE = 512
SUB = 16
LN_ROWS = 32

alpha_scale = 300.0**0.25
norm_eps = 1e-05
masked_score = -1e30
score_scale = HD**-0.5

BF = jnp.bfloat16
F32 = jnp.float32
MESH = pl.DeviceIdType.MESH


def dot(left, right):
    return jnp.dot(left, right, preferred_element_type=F32)


def dot_nt(left, right):
    return lax.dot_general(left, right, (((1,), (1,)), ((), ())), preferred_element_type=F32)


def dot_tn(left, right):
    return lax.dot_general(left, right, (((0,), (0,)), ((), ())), preferred_element_type=F32)


def turned(block):
    return block.astype(F32).T.astype(BF)


def cut(rows):
    units = rows // SUB
    small = (units * 3) // 16
    big = (units - 2 * small + 1) // 2
    sizes = [("xzy", big), ("yzx", units - 2 * small - big), ("zxy", small), ("zyx", small)]
    parts, start = [], 0
    for order, size in sizes:
        if size > 0:
            parts.append((order, start * SUB, size * SUB))
        start += size
    return parts


def slots_of(order, A):
    return 4 * A + 3 if order[0] != "z" else 4 * A + 1


class Layer:
    def __init__(self, A, R, T, parts, refs):
        self.A, self.R, self.T, self.parts = A, R, T, parts
        self.D = 1024
        self.nzx = self.D // (4 * R)
        self.nt = TILE // (2 * R)
        for name, ref in refs.items():
            setattr(self, name, ref)
        self.dp, self.y = lax.axis_index("dp"), lax.axis_index("seq")
        self.c = lax.rem(self.dp, 2)
        self.x = lax.rem(self.dp // 2, 2)
        self.z = self.dp // 4
        self.zx = self.dp // 2
        self.sib = (self.dp + 1 - 2 * self.c, self.y)
        self.near = {"x": (self.dp + 2 - 4 * self.x, self.y), "y": (self.dp, 1 - self.y)}
        self.up = (self.dp + 4, self.y)
        self.down = (self.dp - 4, self.y)
        self.partner = (self.dp - self.c + self.y, self.c)
        self.has_up = self.z < A - 1
        self.has_down = self.z > 0
        self.kept = self.c == self.y
        self.turns = [self.turn(j) for j in range(A)]


    def remote(self, src, dst, send, recv, device):
        return pltpu.make_async_remote_copy(
            src_ref=src, dst_ref=dst, send_sem=send, recv_sem=recv, device_id=device, device_id_type=MESH
        )

    def own(self, axis):
        return self.x if axis == "x" else self.y

    def spot(self, bank, part, z, x, y):
        order, start, rows = self.parts[part]
        row = pl.multiple_of(y * self.R + start, SUB)
        return self.wb.at[bank * 2 * self.A + z * 2 + x, :, pl.ds(row, rows), :]

    def place(self, axis, f, l):
        return (f, l) if axis == "x" else (l, f)


    def barrier(self):
        bar = pltpu.get_barrier_semaphore()

        def greet(device):
            pl.semaphore_signal(bar, inc=1, device_id=device, device_id_type=MESH)

        greet(self.sib)
        greet(self.near["x"])
        greet(self.near["y"])
        for other in range(self.A):

            @pl.when(self.z != other)
            def _():
                greet((self.dp + 4 * (other - self.z), self.y))

        @pl.when(jnp.logical_not(self.kept))
        def _():
            greet(self.partner)
            pl.semaphore_wait(bar, 3 + self.A)

        @pl.when(self.kept)
        def _():
            pl.semaphore_wait(bar, 2 + self.A)


    def ag_index(self, bank, part, z, x, y):
        return ((bank * len(self.parts) + part) * 2 * self.A + z * 2 + x) * 2 + y

    def ag_send(self, bank, part, z, x, y, kind, device):
        ref = self.spot(bank, part, z, x, y)
        slot = (bank * len(self.parts) + part) * 4 + kind
        self.remote(ref, ref, self.ag_s.at[slot], self.ag_r.at[self.ag_index(bank, part, z, x, y)], device).start()

    def ag_wait(self, bank, part, z, x, y):
        ref = self.spot(bank, part, z, x, y)
        self.remote(
            ref, ref, self.ag_s.at[0], self.ag_r.at[self.ag_index(bank, part, z, x, y)], self.sib
        ).wait_recv()

    def ag(self, bank):
        A = self.A
        steps = []
        for part, (order, _, _) in enumerate(self.parts):
            f, l = (order[0], order[2]) if order[0] != "z" else (order[1], order[2])
            steps.append((part, order[0] != "z", f, l, self.own(f), self.own(l)))

        def z_sends(part, f, fc, lc, w, z=None):
            z = self.z if z is None else z
            px, py = self.place(f, fc, lc)

            @pl.when(self.has_up)
            def _():
                self.ag_send(bank, part, z, px, py, w, self.up)

            @pl.when(self.has_down)
            def _():
                self.ag_send(bank, part, z, px, py, w, self.down)

        def send(part, f, fc, lc, z, kind, axis):
            px, py = self.place(f, fc, lc)
            self.ag_send(bank, part, z, px, py, kind, self.near[axis])

        for part, big, f, l, fo, lo in steps:
            if big:
                send(part, f, fo, lo, self.z, 2, f)
            z_sends(part, f, fo, lo, 0)
        for part, big, f, l, fo, lo in steps:
            if not big:
                send(part, f, fo, lo, self.z, 2, f)
            send(part, f, fo, lo, self.z, 3, l)
        yield
        for part, big, f, l, fo, lo in steps:
            px, py = self.place(f, 1 - fo, lo)
            if big:
                self.ag_wait(bank, part, self.z, px, py)
                z_sends(part, f, 1 - fo, lo, 1)
                send(part, f, 1 - fo, lo, self.z, 3, l)
                yield
        for d in range(1, A):
            for part, big, f, l, fo, lo in steps:
                for w in (0, 1) if big else (0,):
                    fc = fo if w == 0 else 1 - fo
                    px, py = self.place(f, fc, lo)

                    def arrived(z, on, device):
                        self.ag_wait(bank, part, z, px, py)

                        @pl.when(on)
                        def _():
                            self.ag_send(bank, part, z, px, py, w, device)

                        if not big:
                            send(part, f, fc, lo, z, 2, f)
                        send(part, f, fc, lo, z, 3, l)

                    @pl.when(self.z >= d)
                    def _():
                        arrived(self.z - d, self.has_up, self.up)

                    @pl.when(self.z + d < A)
                    def _():
                        arrived(self.z + d, self.has_down, self.down)

                    yield
            for part, big, f, l, fo, lo in steps:
                if not big:
                    px, py = self.place(f, 1 - fo, lo)

                    def crossed(z):
                        self.ag_wait(bank, part, z, px, py)
                        send(part, f, 1 - fo, lo, z, 3, l)

                    if d == 1:
                        crossed(self.z)

                    @pl.when(self.z >= d)
                    def _():
                        crossed(self.z - d)

                    @pl.when(self.z + d < A)
                    def _():
                        crossed(self.z + d)

                    yield
        for z in range(A):
            for part, big, f, l, fo, lo in steps:
                for w in (0, 1):
                    px, py = self.place(f, w, 1 - lo)
                    self.ag_wait(bank, part, z, px, py)
            yield

    def ag_drain(self, bank):
        A = self.A
        base = bank * 2 * A
        for part, (order, _, rows) in enumerate(self.parts):
            big = order[0] != "z"

            def sent(kind, count):
                ref = self.wb.at[base : base + count, :, pl.ds(0, rows), :]
                slot = (bank * len(self.parts) + part) * 4 + kind
                self.remote(ref, ref, self.ag_s.at[slot], self.ag_r.at[0], self.sib).wait_send()

            inner = jnp.logical_and(self.has_up, self.has_down)
            for kind in (0, 1) if big else (0,):

                @pl.when(inner)
                def _():
                    sent(kind, A + 1)

                @pl.when(jnp.logical_not(inner))
                def _():
                    sent(kind, 1)

            sent(2, 1 if big else A)
            sent(3, 2 * A)


    def turn(self, j):
        A = self.A
        mirrored = self.z >= A // 2
        w = jnp.where(mirrored, A - 1 - self.z, self.z)
        d = jnp.where(j < A - 1 - w, A - 1 - j, jnp.where(j < A - 1, j - (A - 1 - w), w))
        return jnp.where(mirrored, A - 1 - d, d)

    def rs_land(self, part, slot):
        return self.land[part].at[slot]

    def rs_index(self, part, slot):
        return sum(slots_of(order, self.A) for order, _, _ in self.parts[:part]) + slot

    def rs_send(self, bank, part, z, x, y, slot, kind, device):
        sem = (bank * len(self.parts) + part) * 4 + kind
        self.remote(
            self.spot(bank, part, z, x, y),
            self.rs_land(part, slot),
            self.rs_s.at[sem],
            self.rs_r.at[self.rs_index(part, slot)],
            device,
        ).start()

    def rs_wait(self, part, slot):
        ref = self.rs_land(part, slot)
        self.remote(ref, ref, self.rs_s.at[0], self.rs_r.at[self.rs_index(part, slot)], self.sib).wait_recv()

    def rs_add(self, bank, part, z, x, y, slot, out=None):
        self.rs_wait(part, slot)
        order, start, rows = self.parts[part]
        at = bank * 2 * self.A + z * 2 + x
        row = pl.multiple_of(y * self.R + start, SUB)

        @pl.loop(0, 2)
        def _(h):
            total = self.wb[at, h, pl.ds(row, rows), :].astype(F32) + self.land[part][slot, h].astype(F32)
            if out is None:
                self.wb[at, h, pl.ds(row, rows), :] = total.astype(BF)
            else:
                out[h, start : start + rows, :] = total

    def rs_first(self, bank, z):
        for part, (order, _, _) in enumerate(self.parts):
            l = order[2]
            f = "x" if l == "y" else "y"
            for w in (0, 1):
                px, py = self.place(f, w, 1 - self.own(l))
                self.rs_send(bank, part, z, px, py, z * 2 + w, 3, self.near[l])

    def rs(self, bank, out):
        A = self.A
        info = []
        for part, (order, _, _) in enumerate(self.parts):
            l = order[2]
            f = "x" if l == "y" else "y"
            info.append((part, order[0] != "z", f, l, self.own(f), self.own(l)))

        def chain(part, big, f, fc, lo, w, z, final):
            base = 2 * A + w * (A + 1) if big else 3 * A
            px, py = self.place(f, fc, lo)
            goes_up, goes_down = z > self.z, z < self.z

            def onward(device, next_z, up):
                slot = base + jnp.where(z == next_z, A if not up else z, z)
                self.rs_send(bank, part, z, px, py, slot, w, device)

            @pl.when(goes_up)
            def _():
                @pl.when(self.has_down)
                def _():
                    self.rs_add(bank, part, z, px, py, base + z)

                onward(self.up, self.z + 1, True)

            @pl.when(goes_down)
            def _():
                @pl.when(self.has_up)
                def _():
                    self.rs_add(bank, part, z, px, py, base + z)

                onward(self.down, self.z - 1, False)

            @pl.when(z == self.z)
            def _():
                ends = jnp.logical_and(self.has_down, self.has_up)

                @pl.when(ends)
                def _():
                    self.rs_add(bank, part, z, px, py, base + z)
                    self.rs_add(bank, part, z, px, py, base + A, final)

                @pl.when(jnp.logical_not(ends))
                def _():
                    self.rs_add(bank, part, z, px, py, base + jnp.where(self.has_down, z, A), final)

        for j in range(A):
            z = self.turns[j]
            for part, big, f, l, fo, lo in info:
                for w in (1, 0):
                    fc = fo if w == 0 else 1 - fo
                    px, py = self.place(f, fc, lo)
                    self.rs_add(bank, part, z, px, py, z * 2 + fc)
                    if big:
                        chain(part, big, f, fc, lo, w, z, None)
                    elif w == 1:
                        self.rs_send(bank, part, z, px, py, 2 * A + z, 2, self.near[f])
                    if big:
                        yield
                if not big:
                    yield
            for part, big, f, l, fo, lo in info:
                if not big:
                    px, py = self.place(f, fo, lo)
                    self.rs_add(bank, part, z, px, py, 2 * A + z)
                    chain(part, big, f, fo, lo, 0, z, out if j == A - 1 else None)
                    yield
        for part, big, f, l, fo, lo in info:
            if big:
                px, py = self.place(f, 1 - fo, lo)
                self.rs_send(bank, part, self.z, px, py, 4 * A + 2, 2, self.near[f])
        yield
        for part, big, f, l, fo, lo in info:
            if big:
                px, py = self.place(f, fo, lo)
                self.rs_add(bank, part, self.z, px, py, 4 * A + 2, out)
                yield

    def rs_drain(self, bank):
        A = self.A
        base = bank * 2 * A
        for part, (order, _, rows) in enumerate(self.parts):
            big = order[0] != "z"

            def sent(kind, count):
                ref = self.wb.at[base : base + count, :, pl.ds(0, rows), :]
                slot = (bank * len(self.parts) + part) * 4 + kind
                self.remote(ref, ref, self.rs_s.at[slot], self.rs_r.at[0], self.sib).wait_send()

            sent(0, A - 1)
            if big:
                sent(1, A - 1)
            sent(2, 1 if big else A)
            sent(3, 2 * A)


    def share(self, ref, k):
        rows = ref.at[pl.ds(pl.multiple_of(self.c * self.T, SUB), self.T), :]
        copy = self.remote(rows, rows, self.cg_s.at[k], self.cg_r.at[k], self.sib)
        copy.start()
        return copy

    def shared(self, ref, k):
        rows = ref.at[pl.ds(pl.multiple_of((1 - self.c) * self.T, SUB), self.T), :]
        mine = ref.at[pl.ds(pl.multiple_of(self.c * self.T, SUB), self.T), :]
        self.remote(rows, rows, self.cg_s.at[k], self.cg_r.at[k], self.sib).wait_recv()
        self.remote(mine, mine, self.cg_s.at[k], self.cg_r.at[k], self.sib).wait_send()

    def rows_of(self, which):
        return pl.ds(pl.multiple_of(which * self.T, SUB), self.T)

    def give(self, k, halves):
        buf = k % 2
        for h, value in enumerate(halves(self.rows_of(1 - self.c))):
            self.sb[buf, :, h * TILE : (h + 1) * TILE] = value.astype(BF)
        self.remote(self.sb.at[buf], self.rb.at[buf], self.ex_s.at[k], self.ex_r.at[k], self.sib).start()
        for h, value in enumerate(halves(self.rows_of(self.c))):
            self.pacc[:, h * TILE : (h + 1) * TILE] = value

    def taken(self, k):
        buf = k % 2
        self.remote(self.sb.at[buf], self.rb.at[buf], self.ex_s.at[k], self.ex_r.at[k], self.sib).wait()


    def wcol(self, b):
        return self.wb[pl.ds(b * self.nzx, self.nzx)].reshape(self.D, TILE)

    def wrow(self, b, h):
        return self.wb[pl.ds(b * self.nzx, self.nzx), h].reshape(TILE, TILE)

    def win(self, j, h):
        return self.wb[pl.ds(2 * self.A + j * self.nt, self.nt), h].reshape(TILE, TILE)

    def wout(self, j, h):
        return self.wb[pl.ds(3 * self.A + j * self.nt, self.nt), h].reshape(TILE, TILE)

    def project(self, dst, first, source, block, count):
        @pl.loop(0, count)
        def _(i):
            weight = self.wcol(block + i)
            for m in range(2):
                rows = slice(m * self.T, (m + 1) * self.T)
                dst[first + i, rows, :] = dot(source[rows, :], weight).astype(BF)


    def masks(self):
        lane = lax.broadcasted_iota(jnp.int32, (1, PAIR), 1)
        row = lax.broadcasted_iota(jnp.int32, (PAIR, 1), 0)
        return [(lane < HD), (lane >= HD)], (row < HD)

    def visible(self, tile):
        T = self.T
        key = lax.broadcasted_iota(jnp.int32, (2 * T, T), 0)
        query = lax.broadcasted_iota(jnp.int32, (2 * T, T), 1) + tile * T
        edge = self.pfx_now[0:1, 0:1]
        return jnp.logical_or(key <= query, key.astype(F32) < edge)

    def attend(self, p, qkv, o, lse, masked):
        T = self.T
        cols = pl.ds(pl.multiple_of(p * PAIR, PAIR), PAIR)
        heads, upper = self.masks()
        keys = qkv[1, :, cols]
        values_t = turned(qkv[2, :, cols])
        for tile in range(2):
            rows = slice(tile * T, (tile + 1) * T)
            query = qkv[0, rows, cols].astype(F32) * score_scale
            vis = self.visible(tile) if masked else None
            mixed = []
            for h in range(2):
                scores = dot_nt(keys, jnp.where(heads[h], query, 0.0).astype(BF))
                if masked:
                    scores = jnp.where(vis, scores, masked_score)
                highest = jnp.max(scores, axis=0, keepdims=True)
                exponent = jnp.exp(scores - highest)
                total = jnp.sum(exponent, axis=0, keepdims=True)
                lse[p, h : h + 1, rows] = highest + jnp.log(total)
                mixed.append(dot(values_t, exponent.astype(BF)) * (1.0 / total))
            o[rows, cols] = jnp.where(upper, mixed[0], mixed[1]).T.astype(BF)

    def attend_back(self, p, qkv, do, lse, masked):
        T = self.T
        cols = pl.ds(pl.multiple_of(p * PAIR, PAIR), PAIR)
        heads, upper = self.masks()
        keys, values = qkv[1, :, cols], qkv[2, :, cols]
        keys_t = turned(keys)
        dk = [0.0, 0.0]
        dv = [0.0, 0.0]
        for tile in range(2):
            rows = slice(tile * T, (tile + 1) * T)
            query = qkv[0, rows, cols]
            grad = do[rows, cols]
            query_wide = query.astype(F32) * score_scale
            grad_wide = grad.astype(F32)
            vis = self.visible(tile) if masked else None
            dq = []
            for h in range(2):
                scores = dot_nt(keys, jnp.where(heads[h], query_wide, 0.0).astype(BF))
                if masked:
                    scores = jnp.where(vis, scores, masked_score)
                probs = jnp.exp(scores - lse[p, h : h + 1, rows])
                dprobs = dot_nt(values, jnp.where(heads[h], grad_wide, 0.0).astype(BF))
                delta = jnp.sum(dprobs * probs, axis=0, keepdims=True)
                dscores = (probs * (dprobs - delta)).astype(BF)
                dq.append(dot(keys_t, dscores))
                dk[h] += dot(dscores, query)
                dv[h] += dot(probs.astype(BF), grad)
            self.dqkv[0, rows, cols] = (jnp.where(upper, dq[0], dq[1]) * score_scale).T.astype(BF)
        self.dqkv[1, :, cols] = (jnp.where(heads[0], dk[0], dk[1]) * score_scale).astype(BF)
        self.dqkv[2, :, cols] = jnp.where(heads[0], dv[0], dv[1]).astype(BF)


    def norm(self, summed):
        centred = summed - jnp.mean(summed, axis=-1, keepdims=True)
        inv = lax.rsqrt(jnp.mean(centred * centred, axis=-1, keepdims=True) + norm_eps)
        return centred * inv, inv

    def norm_back(self, k, dy, normed, inv):
        gain = self.norms[k : k + 1, :]
        self.ng[k : k + 1, :] += jnp.sum(dy * normed, axis=0, keepdims=True)
        self.ng[3 + k : 4 + k, :] += jnp.sum(dy, axis=0, keepdims=True)
        scaled = dy * gain
        plain = jnp.mean(scaled, axis=-1, keepdims=True)
        along = jnp.mean(scaled * normed, axis=-1, keepdims=True)
        return inv * (scaled - plain - normed * along)

    def norm_rows(self, body):
        @pl.loop(0, self.T // LN_ROWS)
        def _(i):
            own = pl.ds(pl.multiple_of(i * LN_ROWS, LN_ROWS), LN_ROWS)
            full = pl.ds(pl.multiple_of(self.c * self.T + i * LN_ROWS, LN_ROWS), LN_ROWS)
            body(own, full)


def pump(steps, count):
    for _ in range(count):
        next(steps, None)


def finish(steps):
    for _ in steps:
        pass


def in_loop(steps, index, turns, count):
    for turn in range(turns):

        @pl.when(index == turn)
        def _():
            pump(steps, count)


def kernel(A, R, T, parts, names, *arrays):
    s = Layer(A, R, T, parts, dict(zip(names, arrays)))
    s.land = [getattr(s, f"land{i}") for i in range(len(parts))]
    D = s.D
    away = jnp.logical_not(s.kept)
    s.ng[...] = jnp.zeros_like(s.ng)
    s.barrier()

    block = s.zx // s.nzx
    by_rows = jnp.logical_or(block == 3, block == 7)
    mine = pl.ds(pl.multiple_of(s.y * R, SUB), R)
    ffn_copy = pltpu.make_async_copy(s.ffn_piece, s.wb.at[2 * A + s.zx, :, mine, :], s.lc.at[0])
    ffn_copy.start()
    rows_copy = pltpu.make_async_copy(s.attn_piece, s.wb.at[s.zx, :, mine, :], s.lc.at[1])
    half_copy = pltpu.make_async_copy(s.attn_piece.at[s.c], s.wb.at[s.zx, s.c, mine, :], s.lc.at[2])
    half_send = s.remote(
        s.attn_piece.at[1 - s.c], s.wb.at[s.zx, s.c, mine, :], s.misc_s.at[0], s.misc_r.at[0], s.sib
    )
    half_recv = s.remote(
        s.attn_piece.at[1 - s.c], s.wb.at[s.zx, 1 - s.c, mine, :], s.misc_s.at[0], s.misc_r.at[0], s.sib
    )

    @pl.when(by_rows)
    def _():
        rows_copy.start()

    @pl.when(jnp.logical_not(by_rows))
    def _():
        half_copy.start()
        half_send.start()

    here = s.rows_of(s.c)
    there = s.rows_of(s.y)
    swaps = [
        (s.tokens, s.xf.at[here, :], s.xf.at[there, :]),
        (s.memory, s.mf.at[here, :], s.mf.at[there, :]),
        (s.pfx, s.pfx_now, s.pfx_now),
        (s.cot, s.cotb, s.cotb),
    ]

    @pl.when(s.kept)
    def _():
        for i, (src, dst, _) in enumerate(swaps):
            pltpu.make_async_copy(src, dst, s.lc.at[3 + i]).start()

    @pl.when(away)
    def _():
        for i, (src, _, dst) in enumerate(swaps):
            s.remote(src, dst, s.sw_s.at[i], s.sw_r.at[i], s.partner).start()

    @pl.when(by_rows)
    def _():
        rows_copy.wait()

    @pl.when(jnp.logical_not(by_rows))
    def _():
        half_copy.wait()
        half_send.wait_send()
        half_recv.wait_recv()

    gather = s.ag(0)
    next(gather)

    def swapped(i):
        src, dst, far = swaps[i]

        @pl.when(s.kept)
        def _():
            pltpu.make_async_copy(src, dst, s.lc.at[3 + i]).wait()

        @pl.when(away)
        def _():
            s.remote(src, far, s.sw_s.at[i], s.sw_r.at[i], s.partner).wait_send()
            s.remote(src, dst, s.sw_s.at[i], s.sw_r.at[i], s.partner).wait_recv()

    pump(gather, 4)
    swapped(0)
    s.share(s.xf, 0)
    swapped(1)
    s.share(s.mf, 1)
    swapped(2)
    pump(gather, 24)
    swapped(3)
    s.shared(s.xf, 0)
    s.shared(s.mf, 1)
    ffn_copy.wait()
    ffn = s.ag(1)
    next(ffn)
    finish(gather)

    s.project(s.qkv1, 0, s.xf, 0, 3)
    pump(ffn, 2)
    s.project(s.qkv2, 1, s.mf, 5, 2)
    pump(ffn, 2)

    @pl.loop(0, TILE // PAIR)
    def _(p):
        s.attend(p, s.qkv1, s.o1, s.lse1, True)
        in_loop(ffn, p, TILE // PAIR, 3)

    def branch(o, b):
        return lambda rows: [dot(o[rows, :], s.wrow(b, h)) for h in range(2)]

    s.give(0, branch(s.o1, 3))
    pump(ffn, 1)
    s.taken(0)

    def first_norm(own, full):
        summed = alpha_scale * s.xf[full, :].astype(F32) + s.pacc[own, :] + s.rb[0, own, :].astype(F32)
        normed, inv = s.norm(summed)
        s.dtok[own, :] = normed
        s.inv1[own, :] = inv
        result = normed * s.norms[0:1, :] + s.norms[3:4, :]
        s.nbuf[own, :] = result
        s.n1r[full, :] = result.astype(BF)

    s.norm_rows(first_norm)
    s.share(s.n1r, 2)
    pump(ffn, 2)
    s.shared(s.n1r, 2)

    s.project(s.qkv2, 0, s.n1r, 4, 1)

    @pl.loop(0, TILE // PAIR)
    def _(p):
        s.attend(p, s.qkv2, s.o2, s.lse2, False)
        in_loop(ffn, p, TILE // PAIR, 3)

    s.give(1, branch(s.o2, 7))
    pump(ffn, 1)
    s.taken(1)

    def second_norm(own, full):
        summed = alpha_scale * s.nbuf[own, :] + s.pacc[own, :] + s.rb[1, own, :].astype(F32)
        normed, inv = s.norm(summed)
        s.dmem[own, :] = normed
        s.inv2[own, :] = inv
        result = normed * s.norms[1:2, :] + s.norms[4:5, :]
        s.nbuf[own, :] = result
        s.n2r[full, :] = result.astype(BF)

    s.norm_rows(second_norm)
    s.share(s.n2r, 3)
    pump(ffn, 2)
    s.shared(s.n2r, 3)
    finish(ffn)

    tiles = 2 * A * R // TILE

    @pl.loop(0, tiles)
    def _(j):
        for m in range(2):
            rows = slice(m * T, (m + 1) * T)
            pre = dot_nt(s.n2r[rows, :TILE], s.win(j, 0)) + dot_nt(s.n2r[rows, TILE:], s.win(j, 1))
            gate = 1.0 / (1.0 + jnp.exp(-pre))
            s.act[tiles + j, rows, :] = (pre * gate).astype(BF)
            s.act[j, rows, :] = (gate * (1.0 + pre * (1.0 - gate))).astype(BF)

    def ffn_out(rows):
        return [sum(dot(s.act[tiles + j, rows, :], s.wout(j, h)) for j in range(tiles)) for h in range(2)]

    s.give(2, ffn_out)
    s.taken(2)

    def third_norm(own, full):
        summed = alpha_scale * s.nbuf[own, :] + s.pacc[own, :] + s.rb[0, own, :].astype(F32)
        normed, inv = s.norm(summed)
        result = normed * s.norms[2:3, :] + s.norms[5:6, :]
        s.out[own, :] = result
        s.osb[0, own, :] = result.astype(BF)
        grad = s.norm_back(2, s.cotb[own, :].astype(F32), normed, inv)
        s.nbuf[own, :] = grad
        s.ga[full, :] = grad.astype(BF)

    s.norm_rows(third_norm)
    s.share(s.ga, 4)

    def send_back(k):
        @pl.when(away)
        def _():
            s.remote(s.osb.at[k], s.orb.at[k], s.ob_s.at[k], s.ob_r.at[k], s.partner).start()

    send_back(0)
    s.ag_drain(0)
    s.ag_drain(1)
    s.shared(s.ga, 4)

    @pl.loop(0, tiles)
    def _(j):
        for m in range(2):
            rows = slice(m * T, (m + 1) * T)
            da = dot_nt(s.ga[rows, :TILE], s.wout(j, 0)) + dot_nt(s.ga[rows, TILE:], s.wout(j, 1))
            s.act[j, rows, :] = (da * s.act[j, rows, :].astype(F32)).astype(BF)

    def ffn_in(rows):
        return [sum(dot(s.act[j, rows, :], s.win(j, h)) for j in range(tiles)) for h in range(2)]

    s.give(3, ffn_in)

    @pl.loop(0, tiles)
    def _(j):
        hidden, grads = s.act[tiles + j], s.act[j]
        for h in range(2):
            cols = slice(h * TILE, (h + 1) * TILE)
            out_rows = dot_tn(hidden, s.ga[:, cols]).astype(BF)
            s.wb[pl.ds(3 * A + j * s.nt, s.nt), h] = out_rows.reshape(s.nt, 2 * R, TILE)
            in_rows = dot_tn(grads, s.n2r[:, cols]).astype(BF)
            s.wb[pl.ds(2 * A + j * s.nt, s.nt), h] = in_rows.reshape(s.nt, 2 * R, TILE)

    for j in range(A):
        s.rs_first(1, s.turns[j])
    spread = s.rs(1, s.dffn)
    s.taken(3)

    def second_back(own, full):
        dy = alpha_scale * s.nbuf[own, :] + s.pacc[own, :] + s.rb[1, own, :].astype(F32)
        grad = s.norm_back(1, dy, s.dmem[own, :], s.inv2[own, :])
        s.nbuf[own, :] = grad
        s.gb[full, :] = grad.astype(BF)

    s.norm_rows(second_back)
    s.share(s.gb, 5)
    pump(spread, 2)
    s.shared(s.gb, 5)

    def mixed_back(grad, o, b):
        for m in range(2):
            rows = slice(m * T, (m + 1) * T)
            s.do[rows, :] = (
                dot_nt(grad[rows, :TILE], s.wrow(b, 0)) + dot_nt(grad[rows, TILE:], s.wrow(b, 1))
            ).astype(BF)
        for h in range(2):
            cols = slice(h * TILE, (h + 1) * TILE)
            terms = dot_tn(o[...], grad[:, cols]).astype(BF)
            s.wb[pl.ds(b * s.nzx, s.nzx), h] = terms.reshape(s.nzx, 2 * R, TILE)

    def weight_terms(b, source, grad):
        for h in range(2):
            cols = slice(h * TILE, (h + 1) * TILE)
            terms = dot_tn(source[:, cols], grad).astype(BF)
            half = s.nzx // 2 if s.nzx > 1 else 0
            if half:
                s.wb[pl.ds(b * s.nzx + h * half, half)] = terms.reshape(half, 2, 2 * R, TILE)
            else:
                s.wb[b, h] = terms

    def spread_back(rows, blocks):
        halves = []
        for h in range(2):
            total = 0.0
            for b, k in blocks:
                total += dot_nt(s.dqkv[k, rows, :], s.wcol(b)[h * TILE : (h + 1) * TILE])
            halves.append(total)
        return halves

    mixed_back(s.gb, s.o2, 7)
    pump(spread, 2)

    @pl.loop(0, TILE // PAIR)
    def _(p):
        s.attend_back(p, s.qkv2, s.do, s.lse2, False)
        in_loop(spread, p, TILE // PAIR, 3)

    s.give(4, lambda rows: spread_back(rows, [(5, 1), (6, 2)]))
    pump(spread, 1)
    s.taken(4)

    def memory_rows(own, full):
        total = s.pacc[own, :] + s.rb[0, own, :].astype(F32)
        s.dmem[own, :] = total
        s.osb[1, own, :] = total.astype(BF)

    s.norm_rows(memory_rows)
    send_back(1)
    s.give(5, lambda rows: spread_back(rows, [(4, 0)]))
    pump(spread, 1)
    weight_terms(4, s.n1r, s.dqkv[0])
    weight_terms(5, s.mf, s.dqkv[1])
    weight_terms(6, s.mf, s.dqkv[2])
    pump(spread, 1)
    s.taken(5)

    def first_back(own, full):
        dy = alpha_scale * s.nbuf[own, :] + s.pacc[own, :] + s.rb[1, own, :].astype(F32)
        grad = s.norm_back(0, dy, s.dtok[own, :], s.inv1[own, :])
        s.nbuf[own, :] = grad
        s.ga[full, :] = grad.astype(BF)

    s.norm_rows(first_back)
    s.share(s.ga, 6)
    pump(spread, 2)
    s.shared(s.ga, 6)

    def norm_sum():
        for k, device in enumerate((s.sib, s.near["x"], s.near["y"])):
            copy = s.remote(s.ngs.at[k], s.ngr.at[k], s.nm_s.at[k], s.nm_r.at[k], device)
            s.ngs[k] = s.ng[...]
            copy.start()
            yield
            copy.wait()
            s.ng[...] = s.ng[...] + s.ngr[k]
        s.ngz[s.z] = s.ng[...]
        for other in range(A):

            @pl.when(s.z != other)
            def _():
                s.remote(
                    s.ng, s.ngz.at[s.z], s.nm_s.at[3 + other], s.nm_r.at[3 + s.z],
                    (s.dp + 4 * (other - s.z), s.y),
                ).start()

        yield
        for other in range(A):

            @pl.when(s.z != other)
            def _():
                s.remote(s.ng, s.ngz.at[other], s.nm_s.at[3 + other], s.nm_r.at[3 + other], s.sib).wait()

        total = s.ngz[0]
        for other in range(1, A):
            total = total + s.ngz[other]
        s.dnorm[...] = total[:6, :]
        yield

    sums = norm_sum()
    next(sums)

    mixed_back(s.ga, s.o1, 3)
    pump(spread, 2)
    next(sums)

    @pl.loop(0, TILE // PAIR)
    def _(p):
        s.attend_back(p, s.qkv1, s.do, s.lse1, True)
        in_loop(spread, p, TILE // PAIR, 4)

    next(sums)
    s.give(6, lambda rows: spread_back(rows, [(0, 0), (1, 1), (2, 2)]))
    next(sums)

    @pl.loop(0, 3)
    def _(k):
        weight_terms(k, s.xf, s.dqkv[k])

    finish(sums)
    s.taken(6)

    def token_rows(own, full):
        total = alpha_scale * s.nbuf[own, :] + s.pacc[own, :] + s.rb[0, own, :].astype(F32)
        s.dtok[own, :] = total
        s.osb[2, own, :] = total.astype(BF)

    s.norm_rows(token_rows)
    send_back(2)
    finish(spread)

    for k, device in enumerate((s.near["x"], s.near["y"])):
        pl.semaphore_signal(s.credit.at[k], inc=1, device_id=device, device_id_type=MESH)

    @pl.when(s.has_up)
    def _():
        pl.semaphore_signal(s.credit.at[2], inc=1, device_id=s.up, device_id_type=MESH)

    @pl.when(s.has_down)
    def _():
        pl.semaphore_signal(s.credit.at[3], inc=1, device_id=s.down, device_id_type=MESH)

    pl.semaphore_wait(s.credit.at[0], 1)
    pl.semaphore_wait(s.credit.at[1], 1)

    @pl.when(s.has_down)
    def _():
        pl.semaphore_wait(s.credit.at[2], 1)

    @pl.when(s.has_up)
    def _():
        pl.semaphore_wait(s.credit.at[3], 1)

    for j in range(A):
        s.rs_first(0, s.turns[j])

    @pl.when(away)
    def _():
        for k, dst in enumerate((s.out, s.dmem, s.dtok)):
            s.remote(s.osb.at[k], s.orb.at[k], s.ob_s.at[k], s.ob_r.at[k], s.partner).wait()

            @pl.loop(0, T // LN_ROWS)
            def _(i):
                own = pl.ds(pl.multiple_of(i * LN_ROWS, LN_ROWS), LN_ROWS)
                dst[own, :] = s.orb[k, own, :].astype(F32)

    finish(s.rs(0, s.fin))

    tail_send = s.remote(s.fin.at[1 - s.c], s.dattn.at[s.c], s.misc_s.at[1], s.misc_r.at[1], s.sib)
    tail_recv = s.remote(s.fin.at[1 - s.c], s.dattn.at[1 - s.c], s.misc_s.at[1], s.misc_r.at[1], s.sib)

    @pl.when(by_rows)
    def _():
        s.dattn[...] = s.fin[...]

    @pl.when(jnp.logical_not(by_rows))
    def _():
        tail_send.start()
        s.dattn[s.c] = s.fin[s.c]
        tail_send.wait_send()
        tail_recv.wait_recv()

    s.rs_drain(1)
    s.rs_drain(0)


def on_device(A, tokens, memory, attn_bank, ffn_bank, norm_params, prefix, cotangent):
    T, D = tokens.shape
    R = attn_bank.shape[0]
    parts = cut(R)
    groups = D // (4 * R)
    tiles = 2 * A * R // TILE

    def by_half(shard):
        return shard.reshape(R, 2, TILE).transpose(1, 0, 2)

    def by_core(shard):
        return shard.reshape(R, groups, 2, 2 * R).transpose(2, 0, 1, 3).reshape(2, R, TILE)

    block = (lax.axis_index("dp") // 2) // groups
    by_rows = jnp.logical_or(block == 3, block == 7)
    attn_piece = by_half(attn_bank)
    if groups > 1:
        attn_piece = jnp.where(by_rows, attn_piece, by_core(attn_bank))
    pfx = jnp.broadcast_to(prefix.astype(F32)[0], (8, 128))
    np_ = len(parts)
    slots = sum(slots_of(order, A) for order, _, _ in parts)

    inputs = dict(
        tokens=tokens,
        memory=memory,
        cot=cotangent,
        pfx=pfx,
        attn_piece=attn_piece,
        ffn_piece=by_half(ffn_bank),
        norms=norm_params,
    )
    in_vmem = ("pfx", "norms")
    outputs = dict(
        out=(T, D), dtok=(T, D), dmem=(T, D), dattn=(2, R, TILE), dffn=(2, R, TILE), dnorm=(6, D)
    )
    wide = lambda *shape: pltpu.VMEM(shape, F32)
    low = lambda *shape: pltpu.VMEM(shape, BF)
    dma = lambda count: pltpu.SemaphoreType.DMA((count,))
    scratch = dict(
        wb=low(4 * A, 2, 2 * R, TILE),
        xf=low(2 * T, D),
        mf=low(2 * T, D),
        n1r=low(2 * T, D),
        n2r=low(2 * T, D),
        ga=low(2 * T, D),
        gb=low(2 * T, D),
        cotb=low(T, D),
        act=low(2 * tiles, 2 * T, TILE),
        qkv1=low(3, 2 * T, TILE),
        qkv2=low(3, 2 * T, TILE),
        dqkv=low(3, 2 * T, TILE),
        o1=low(2 * T, TILE),
        o2=low(2 * T, TILE),
        do=low(2 * T, TILE),
        sb=low(2, T, D),
        rb=low(2, T, D),
        osb=low(3, T, D),
        orb=low(3, T, D),
        nbuf=wide(T, D),
        pacc=wide(T, D),
        fin=wide(2, R, TILE),
        pfx_now=wide(8, 128),
        lse1=wide(TILE // PAIR, 8, 2 * T),
        lse2=wide(TILE // PAIR, 8, 2 * T),
        inv1=wide(T, 1),
        inv2=wide(T, 1),
        ng=wide(8, D),
        ngs=wide(3, 8, D),
        ngr=wide(3, 8, D),
        ngz=wide(A, 8, D),
        lc=dma(7),
        misc_s=dma(2),
        misc_r=dma(2),
        sw_s=dma(4),
        sw_r=dma(4),
        ag_s=dma(2 * np_ * 4),
        ag_r=dma(2 * np_ * 4 * A),
        rs_s=dma(2 * np_ * 4),
        rs_r=dma(slots),
        cg_s=dma(7),
        cg_r=dma(7),
        ex_s=dma(7),
        ex_r=dma(7),
        ob_s=dma(3),
        ob_r=dma(3),
        nm_s=dma(3 + A),
        nm_r=dma(3 + A),
        credit=pltpu.SemaphoreType.REGULAR((4,)),
    )
    for i, (order, _, rows) in enumerate(parts):
        scratch[f"land{i}"] = low(slots_of(order, A), 2, rows, TILE)
    names = list(inputs) + list(outputs) + list(scratch)
    out, dtok, dmem, dattn, dffn, dnorm = pl.pallas_call(
        functools.partial(kernel, A, R, T, parts, names),
        out_shape=[jax.ShapeDtypeStruct(shape, F32) for shape in outputs.values()],
        in_specs=[pl.BlockSpec(memory_space=pltpu.VMEM if n in in_vmem else pl.ANY) for n in inputs],
        out_specs=[pl.BlockSpec(memory_space=pltpu.VMEM)] * len(outputs),
        scratch_shapes=list(scratch.values()),
        compiler_params=pltpu.CompilerParams(
            collective_id=0, has_side_effects=True, vmem_limit_bytes=64 * 2**20
        ),
        name="layer",
    )(*inputs.values())

    def half_back(pieces):
        return pieces.transpose(1, 0, 2).reshape(R, D)

    def core_back(pieces):
        return pieces.reshape(2, R, groups, 2 * R).transpose(1, 2, 0, 3).reshape(R, D)

    attn_rows = half_back(dattn)
    if groups > 1:
        attn_rows = jnp.where(by_rows, attn_rows, core_back(dattn))
    return (out, dtok, dmem, attn_rows, half_back(dffn), dnorm)


def solution(mesh):
    rows = P(("dp", "seq"), None)
    return jax.shard_map(
        functools.partial(on_device, mesh.shape["dp"] // 4),
        mesh=mesh,
        in_specs=(rows, rows, rows, rows, P(), P("dp"), rows),
        out_specs=(rows, rows, rows, rows, rows, P()),
        check_vma=False,
    )
```

time: 2040 us -> 430 us (0.21)
  waiting for transfers between devices: 1600 us -> 0 us
  Pallas kernels: 0 us -> 410 us
  matrix products: 154 us -> 0 us
  local copies, waits for them, and re-layouts: 152 us -> 13.4 us
  blocking collectives: 46.9 us -> 0 us
  other arithmetic: 32.2 us -> 0 us
  loops' own time: 22.6 us -> 0 us
    reduce_scatter x6 -> x0, waiting for transfers between devices: 1380 us -> none  [the longest x1 710 us: on_device(): lax.psum_scatter(attn_terms, ('dp', 'seq'), scatter_dimension=0, tiled=True)]
    pallas_call x0 -> x1, Pallas kernels: none -> 410 us  [on_device(): pl.pallas_call(functools.partial(kernel, A, R, T, parts, names), out_shap...]
    all_gather x6 -> x0, waiting for transfers between devices: 219 us -> none  [the longest x1 121 us: on_device(): lax.all_gather(attn_bank, ('dp', 'seq'), axis=0, tiled=True)]
    dot_general x142 -> x0, matrix products: 154 us -> none  [the longest x10 41.5 us: matmul_tn(): lax.dot_general(left, right, (((0,), (0,)), ((), ())), preferred_element_...]
    dynamic_slice x144 -> x0, local copies, waits for them, and re-layouts: 98.7 us -> none  [the longest x32 27.2 us: one_group(): lax.dynamic_slice_in_dim(queries, column, group_width, 1)]
    psum x1 -> x0, blocking collectives: 46.9 us -> none  [on_device(): norm_grad = lax.psum(norm_terms, ('dp', 'seq'))]
    dynamic_update_slice x48 -> x0, local copies, waits for them, and re-layouts: 31.6 us -> none  [the longest x16 11.5 us: one_group(): lax.dynamic_update_slice_in_dim(value_acc, value_piece.reshape(key_count,...]
    another operation x4 -> x0, loops' own time: 22.6 us -> none  [the longest x2 11.7 us: attend_back(): lax.scan(one_group, initial, (jnp.arange(model_width // group_width), log...]
  transfers between devices with their start and end apart: 12 -> 0, of which waited for: 8 -> 0; matrix products, arithmetic and copies ran while one was open for 8% -> 0% of each run, Pallas kernels for 0% -> 0%
where the time goes in v1:
time: 430 us; the launch traced here: 425 us
  Pallas kernels  410 us (95%)
  local copies, waits for them, and re-layouts  13.4 us (3%)
    pallas_call x1, Pallas kernels, on_device(): pl.pallas_call(functools.partial(kernel, A, R, T, parts, names), out_shap...  410 us
    unnamed x20, local copies, waits for them, and re-layouts  8.89 us

profile of v1, /device:TPU:0, one launch (start us, length us, event | category | flops | bytes accessed | tf_op | source)
XLA Modules:
  0.0 424.8 jit_solution(16695977318203277908)
XLA Ops:
  1.3 0.6 broadcast_in_dim.3.arrays_3_
  1.9 1.2 copy.13
  3.1 0.0 copy-start.4
  3.1 1.0 copy.14
  4.1 0.0 copy-done.4
  4.2 0.2 copy.15
  4.4 1.0 copy.16
  5.4 409.6 %layer.1 = (f32[256,1024]{1,0:T(8,128)}, f32[256,1024]{1,0:T(8,128)}, f32[256,1024]{1,0:T(8,128)}, f32[2,256,512]{2,1,0:T(8,128)}, f32[2,256,512]{2,1,0:T(8,128)}, /*index=5*/f32[6,1024]{1,0:T(8,128)}) custom-call(bf16[256,1024]{1,0:T(8,128)(2,1)} %arrays_0_.1, bf16[256,1024]{1,0:T(8,128)(2,1)} %arrays_1_.1, bf16[256,1024]{1,0:T(8,128)(2,1)} %arrays_2_.1, ...), custom_call_target="tpu_custom_call" | custom-call | tf_op jit(solution)/shard_map/layer/pallas_call | solution.py:1060
  415.0 1.6 copy.17
  416.6 0.0 copy-start.3
  416.6 1.3 copy.19
  417.9 0.0 copy-done.3
  417.9 0.3 copy.18
  418.2 0.0 copy-start.2
  418.2 1.3 copy.20
  419.6 0.0 copy-done.2
  419.6 0.0 copy-start.1
  419.6 1.0 copy.26
  420.5 0.6 copy-done.1
  421.2 0.0 copy-start
  421.2 1.0 copy.27
  422.1 0.6 copy-done
  422.8 0.0 copy-start.5
  422.8 1.0 copy.28
  423.7 0.0 copy-done.5
  423.7 0.6 copy.29
Async XLA Ops:
  3.1 1.0 copy-start.4
  416.6 1.3 copy-start.3
  418.2 1.3 copy-start.2
  419.6 1.6 copy-start.1
  421.2 1.6 copy-start
  422.8 1.0 copy-start.5

commit v2 on v1

--- a/solution.py
+++ b/solution.py
@@ -12,6 +12,9 @@
 TILE = 512
 SUB = 16
 LN_ROWS = 32
+AHEAD = 8
+GATHER = (5, 5, 3, 3)
+SCATTER = (5, 5, 3, 3)
 
 alpha_scale = 300.0**0.25
 norm_eps = 1e-05
@@ -39,11 +42,10 @@
     return block.astype(F32).T.astype(BF)
 
 
-def cut(rows):
+def cut(rows, split):
     units = rows // SUB
-    small = (units * 3) // 16
-    big = (units - 2 * small + 1) // 2
-    sizes = [("xzy", big), ("yzx", units - 2 * small - big), ("zxy", small), ("zyx", small)]
+    shares = [(units * share + 8) // 16 for share in split[1:]]
+    sizes = list(zip(("xzy", "yzx", "zxy", "zyx"), [units - sum(shares)] + shares))
     parts, start = [], 0
     for order, size in sizes:
         if size > 0:
@@ -57,8 +59,9 @@
 
 
 class Layer:
-    def __init__(self, A, R, T, parts, refs):
-        self.A, self.R, self.T, self.parts = A, R, T, parts
+    def __init__(self, A, R, T, ag_parts, rs_parts, refs):
+        self.A, self.R, self.T = A, R, T
+        self.ag_parts, self.rs_parts = ag_parts, rs_parts
         self.D = 1024
         self.nzx = self.D // (4 * R)
         self.nt = TILE // (2 * R)
@@ -89,7 +92,7 @@
         return self.x if axis == "x" else self.y
 
     def spot(self, bank, part, z, x, y):
-        order, start, rows = self.parts[part]
+        order, start, rows = part
         row = pl.multiple_of(y * self.R + start, SUB)
         return self.wb.at[bank * 2 * self.A + z * 2 + x, :, pl.ds(row, rows), :]
 
@@ -123,120 +126,139 @@
 
 
     def ag_index(self, bank, part, z, x, y):
-        return ((bank * len(self.parts) + part) * 2 * self.A + z * 2 + x) * 2 + y
+        return ((bank * len(self.ag_parts) + part) * 2 * self.A + z * 2 + x) * 2 + y
 
     def ag_send(self, bank, part, z, x, y, kind, device):
-        ref = self.spot(bank, part, z, x, y)
-        slot = (bank * len(self.parts) + part) * 4 + kind
+        ref = self.spot(bank, self.ag_parts[part], z, x, y)
+        slot = (bank * len(self.ag_parts) + part) * 4 + kind
         self.remote(ref, ref, self.ag_s.at[slot], self.ag_r.at[self.ag_index(bank, part, z, x, y)], device).start()
 
     def ag_wait(self, bank, part, z, x, y):
-        ref = self.spot(bank, part, z, x, y)
+        ref = self.spot(bank, self.ag_parts[part], z, x, y)
         self.remote(
             ref, ref, self.ag_s.at[0], self.ag_r.at[self.ag_index(bank, part, z, x, y)], self.sib
         ).wait_recv()
 
     def ag(self, bank):
         A = self.A
-        steps = []
-        for part, (order, _, _) in enumerate(self.parts):
-            f, l = (order[0], order[2]) if order[0] != "z" else (order[1], order[2])
-            steps.append((part, order[0] != "z", f, l, self.own(f), self.own(l)))
-
-        def z_sends(part, f, fc, lc, w, z=None):
-            z = self.z if z is None else z
+        info, steps = self.orders(self.ag_parts), []
+
+        def z_sends(part, f, fc, lc, w):
             px, py = self.place(f, fc, lc)
 
             @pl.when(self.has_up)
             def _():
-                self.ag_send(bank, part, z, px, py, w, self.up)
+                self.ag_send(bank, part, self.z, px, py, w, self.up)
 
             @pl.when(self.has_down)
             def _():
-                self.ag_send(bank, part, z, px, py, w, self.down)
+                self.ag_send(bank, part, self.z, px, py, w, self.down)
 
         def send(part, f, fc, lc, z, kind, axis):
             px, py = self.place(f, fc, lc)
             self.ag_send(bank, part, z, px, py, kind, self.near[axis])
 
-        for part, big, f, l, fo, lo in steps:
-            if big:
-                send(part, f, fo, lo, self.z, 2, f)
-            z_sends(part, f, fo, lo, 0)
-        for part, big, f, l, fo, lo in steps:
-            if not big:
-                send(part, f, fo, lo, self.z, 2, f)
-            send(part, f, fo, lo, self.z, 3, l)
-        yield
-        for part, big, f, l, fo, lo in steps:
+        def early():
+            for part, big, f, l, fo, lo in info:
+                if big:
+                    send(part, f, fo, lo, self.z, 2, f)
+
+        def begin():
+            for part, big, f, l, fo, lo in info:
+                z_sends(part, f, fo, lo, 0)
+            for part, big, f, l, fo, lo in info:
+                if not big:
+                    send(part, f, fo, lo, self.z, 2, f)
+                send(part, f, fo, lo, self.z, 3, l)
+
+        def beside(part, big, f, l, fo, lo):
             px, py = self.place(f, 1 - fo, lo)
-            if big:
-                self.ag_wait(bank, part, self.z, px, py)
-                z_sends(part, f, 1 - fo, lo, 1)
-                send(part, f, 1 - fo, lo, self.z, 3, l)
-                yield
+            self.ag_wait(bank, part, self.z, px, py)
+            z_sends(part, f, 1 - fo, lo, 1)
+            send(part, f, 1 - fo, lo, self.z, 3, l)
+
+        def arrive(d, w, part, big, f, l, fo, lo):
+            fc = fo if w == 0 else 1 - fo
+            px, py = self.place(f, fc, lo)
+
+            def arrived(z, on, device):
+                self.ag_wait(bank, part, z, px, py)
+
+                @pl.when(on)
+                def _():
+                    self.ag_send(bank, part, z, px, py, w, device)
+
+                if not big:
+                    send(part, f, fc, lo, z, 2, f)
+                send(part, f, fc, lo, z, 3, l)
+
+            @pl.when(self.z >= d)
+            def _():
+                arrived(self.z - d, self.has_up, self.up)
+
+            @pl.when(self.z + d < A)
+            def _():
+                arrived(self.z + d, self.has_down, self.down)
+
+        def cross(d, part, big, f, l, fo, lo):
+            px, py = self.place(f, 1 - fo, lo)
+
+            def crossed(z):
+                self.ag_wait(bank, part, z, px, py)
+                send(part, f, 1 - fo, lo, z, 3, l)
+
+            self.planes_at(d, crossed)
+
+        def end(d, w, part, big, f, l, fo, lo):
+            px, py = self.place(f, w, 1 - lo)
+            self.planes_at(d, lambda z: self.ag_wait(bank, part, z, px, py))
+
+        bigs = [row for row in info if row[1]]
+        smalls = [row for row in info if not row[1]]
+        steps += [early, begin]
         for d in range(1, A):
-            for part, big, f, l, fo, lo in steps:
-                for w in (0, 1) if big else (0,):
-                    fc = fo if w == 0 else 1 - fo
-                    px, py = self.place(f, fc, lo)
-
-                    def arrived(z, on, device):
-                        self.ag_wait(bank, part, z, px, py)
-
-                        @pl.when(on)
-                        def _():
-                            self.ag_send(bank, part, z, px, py, w, device)
-
-                        if not big:
-                            send(part, f, fc, lo, z, 2, f)
-                        send(part, f, fc, lo, z, 3, l)
-
-                    @pl.when(self.z >= d)
-                    def _():
-                        arrived(self.z - d, self.has_up, self.up)
-
-                    @pl.when(self.z + d < A)
-                    def _():
-                        arrived(self.z + d, self.has_down, self.down)
-
-                    yield
-            for part, big, f, l, fo, lo in steps:
-                if not big:
-                    px, py = self.place(f, 1 - fo, lo)
-
-                    def crossed(z):
-                        self.ag_wait(bank, part, z, px, py)
-                        send(part, f, 1 - fo, lo, z, 3, l)
-
-                    if d == 1:
-                        crossed(self.z)
-
-                    @pl.when(self.z >= d)
-                    def _():
-                        crossed(self.z - d)
-
-                    @pl.when(self.z + d < A)
-                    def _():
-                        crossed(self.z + d)
-
-                    yield
-        for z in range(A):
-            for part, big, f, l, fo, lo in steps:
+            steps += [functools.partial(arrive, d, 0, *row) for row in info]
+            if d == 1:
+                steps += [functools.partial(beside, *row) for row in bigs]
+            steps += [functools.partial(arrive, d, 1, *row) for row in bigs]
+            steps += [functools.partial(cross, d - 1, *row) for row in smalls]
+        steps += [functools.partial(cross, A - 1, *row) for row in smalls]
+        for d in range(A):
+            for row in info:
                 for w in (0, 1):
-                    px, py = self.place(f, w, 1 - lo)
-                    self.ag_wait(bank, part, z, px, py)
-            yield
+                    steps.append(functools.partial(end, d, w, *row))
+        return steps
+
+    def planes_at(self, d, act):
+        if d == 0:
+            act(self.z)
+            return
+
+        @pl.when(self.z >= d)
+        def _():
+            act(self.z - d)
+
+        @pl.when(self.z + d < self.A)
+        def _():
+            act(self.z + d)
+
+    def orders(self, parts):
+        info = []
+        for part, (order, _, _) in enumerate(parts):
+            l = order[2]
+            f = "x" if l == "y" else "y"
+            info.append((part, order[0] != "z", f, l, self.own(f), self.own(l)))
+        return info
 
     def ag_drain(self, bank):
         A = self.A
         base = bank * 2 * A
-        for part, (order, _, rows) in enumerate(self.parts):
+        for part, (order, _, rows) in enumerate(self.ag_parts):
             big = order[0] != "z"
 
             def sent(kind, count):
                 ref = self.wb.at[base : base + count, :, pl.ds(0, rows), :]
-                slot = (bank * len(self.parts) + part) * 4 + kind
+                slot = (bank * len(self.ag_parts) + part) * 4 + kind
                 self.remote(ref, ref, self.ag_s.at[slot], self.ag_r.at[0], self.sib).wait_send()
 
             inner = jnp.logical_and(self.has_up, self.has_down)
@@ -261,135 +283,218 @@
         d = jnp.where(j < A - 1 - w, A - 1 - j, jnp.where(j < A - 1, j - (A - 1 - w), w))
         return jnp.where(mirrored, A - 1 - d, d)
 
-    def rs_land(self, part, slot):
+    def rs_land(self, bank, part, slot, first):
+        if bank == 0 and first:
+            _, start, rows = self.rs_parts[part]
+            return self.act.at[slot, :, start : start + rows, :]
         return self.land[part].at[slot]
 
-    def rs_index(self, part, slot):
-        return sum(slots_of(order, self.A) for order, _, _ in self.parts[:part]) + slot
+    def rs_index(self, bank, part, slot, first):
+        slots = [slots_of(order, self.A) + 3 for order, _, _ in self.rs_parts]
+        group = 0 if bank == 1 else 1 if first else 2
+        return group * sum(slots) + sum(slots[:part]) + slot
 
     def rs_send(self, bank, part, z, x, y, slot, kind, device):
-        sem = (bank * len(self.parts) + part) * 4 + kind
+        sem = (bank * len(self.rs_parts) + part) * 4 + kind
         self.remote(
-            self.spot(bank, part, z, x, y),
-            self.rs_land(part, slot),
+            self.spot(bank, self.rs_parts[part], z, x, y),
+            self.rs_land(bank, part, slot, kind == 3),
             self.rs_s.at[sem],
-            self.rs_r.at[self.rs_index(part, slot)],
+            self.rs_r.at[self.rs_index(bank, part, slot, kind == 3)],
             device,
         ).start()
 
-    def rs_wait(self, part, slot):
-        ref = self.rs_land(part, slot)
-        self.remote(ref, ref, self.rs_s.at[0], self.rs_r.at[self.rs_index(part, slot)], self.sib).wait_recv()
-
-    def rs_add(self, bank, part, z, x, y, slot, out=None):
-        self.rs_wait(part, slot)
-        order, start, rows = self.parts[part]
+    def rs_add(self, bank, part, z, x, y, slot, out=None, first=False):
+        landed = self.rs_land(bank, part, slot, first)
+        self.remote(
+            landed, landed, self.rs_s.at[0], self.rs_r.at[self.rs_index(bank, part, slot, first)], self.sib
+        ).wait_recv()
+        order, start, rows = self.rs_parts[part]
         at = bank * 2 * self.A + z * 2 + x
         row = pl.multiple_of(y * self.R + start, SUB)
 
         @pl.loop(0, 2)
         def _(h):
-            total = self.wb[at, h, pl.ds(row, rows), :].astype(F32) + self.land[part][slot, h].astype(F32)
+            total = self.wb[at, h, pl.ds(row, rows), :].astype(F32) + landed[h].astype(F32)
             if out is None:
                 self.wb[at, h, pl.ds(row, rows), :] = total.astype(BF)
             else:
                 out[h, start : start + rows, :] = total
 
-    def rs_first(self, bank, z):
-        for part, (order, _, _) in enumerate(self.parts):
-            l = order[2]
-            f = "x" if l == "y" else "y"
-            for w in (0, 1):
-                px, py = self.place(f, w, 1 - self.own(l))
-                self.rs_send(bank, part, z, px, py, z * 2 + w, 3, self.near[l])
-
-    def rs(self, bank, out):
+    def rs_firsts(self, bank):
+        sends = []
+
+        def send(z, w, part, big, f, l, fo, lo):
+            fc = fo if w == 0 else 1 - fo
+            px, py = self.place(f, fc, 1 - lo)
+            self.rs_send(bank, part, z, px, py, z * 2 + fc, 3, self.near[l])
+
+        for z in self.turns:
+            for row in self.orders(self.rs_parts):
+                for w in (1, 0):
+                    sends.append(functools.partial(send, z, w, *row))
+        return sends
+
+    def rs_slot(self, bank, part, slot):
+        if bank == 1:
+            return slot
         A = self.A
-        info = []
-        for part, (order, _, _) in enumerate(self.parts):
-            l = order[2]
-            f = "x" if l == "y" else "y"
-            info.append((part, order[0] != "z", f, l, self.own(f), self.own(l)))
-
-        def chain(part, big, f, fc, lo, w, z, final):
-            base = 2 * A + w * (A + 1) if big else 3 * A
+        more = slots_of(self.rs_parts[part][0], A)
+        slot = slot - 2 * A
+        return jnp.where(slot < 2 * A, slot, slot - 2 * A + more)
+
+    def chain(self, bank, part, big, f, fc, lo, w, z, final):
+        A = self.A
+        base = 2 * A + w * (A + 1) if big else 3 * A
+        px, py = self.place(f, fc, lo)
+
+        def slot(k):
+            return self.rs_slot(bank, part, base + k)
+
+        def onward(device, next_z, up):
+            self.rs_send(bank, part, z, px, py, slot(z if up else jnp.where(z == next_z, A, z)), w, device)
+
+        @pl.when(z > self.z)
+        def _():
+            @pl.when(self.has_down)
+            def _():
+                self.rs_add(bank, part, z, px, py, slot(z))
+
+            onward(self.up, self.z + 1, True)
+
+        @pl.when(z < self.z)
+        def _():
+            @pl.when(self.has_up)
+            def _():
+                self.rs_add(bank, part, z, px, py, slot(z))
+
+            onward(self.down, self.z - 1, False)
+
+        @pl.when(z == self.z)
+        def _():
+            inner = jnp.logical_and(self.has_down, self.has_up)
+
+            @pl.when(inner)
+            def _():
+                self.rs_add(bank, part, z, px, py, slot(z))
+                self.rs_add(bank, part, z, px, py, slot(A), final)
+
+            @pl.when(jnp.logical_not(inner))
+            def _():
+                self.rs_add(bank, part, z, px, py, slot(jnp.where(self.has_down, z, A)), final)
+
+    def rs_across(self, bank, j, sends):
+        A, z = self.A, self.turns[j]
+
+        def across(w, more, part, big, f, l, fo, lo):
+            fc = fo if w == 0 else 1 - fo
             px, py = self.place(f, fc, lo)
-            goes_up, goes_down = z > self.z, z < self.z
-
-            def onward(device, next_z, up):
-                slot = base + jnp.where(z == next_z, A if not up else z, z)
-                self.rs_send(bank, part, z, px, py, slot, w, device)
-
-            @pl.when(goes_up)
-            def _():
-                @pl.when(self.has_down)
-                def _():
-                    self.rs_add(bank, part, z, px, py, base + z)
-
-                onward(self.up, self.z + 1, True)
-
-            @pl.when(goes_down)
-            def _():
-                @pl.when(self.has_up)
-                def _():
-                    self.rs_add(bank, part, z, px, py, base + z)
-
-                onward(self.down, self.z - 1, False)
-
-            @pl.when(z == self.z)
-            def _():
-                ends = jnp.logical_and(self.has_down, self.has_up)
-
-                @pl.when(ends)
-                def _():
-                    self.rs_add(bank, part, z, px, py, base + z)
-                    self.rs_add(bank, part, z, px, py, base + A, final)
-
-                @pl.when(jnp.logical_not(ends))
-                def _():
-                    self.rs_add(bank, part, z, px, py, base + jnp.where(self.has_down, z, A), final)
-
+            self.rs_add(bank, part, z, px, py, z * 2 + fc, first=True)
+            if more:
+                more()
+            if w == 1 and not big:
+                self.rs_send(bank, part, z, px, py, self.rs_slot(bank, part, 2 * A + z), 2, self.near[f])
+
+        return [
+            functools.partial(across, w, sends.pop(0) if sends else None, *row)
+            for row in self.orders(self.rs_parts)
+            for w in (1, 0)
+        ]
+
+    def rs_along(self, bank, j, out, bigs):
+        A, z = self.A, self.turns[j]
+
+        def along(w, part, big, f, l, fo, lo):
+            if big:
+                self.chain(bank, part, big, f, fo if w == 0 else 1 - fo, lo, w, z, None)
+            else:
+                px, py = self.place(f, fo, lo)
+                self.rs_add(bank, part, z, px, py, self.rs_slot(bank, part, 2 * A + z))
+                self.chain(bank, part, big, f, fo, lo, 0, z, out if j == A - 1 else None)
+
+        return [
+            functools.partial(along, w, *row)
+            for row in self.orders(self.rs_parts)
+            if row[1] == bigs
+            for w in ((1, 0) if bigs else (0,))
+        ]
+
+    def rs_last(self, bank, out):
+        A = self.A
+
+        def go():
+            for part, big, f, l, fo, lo in self.orders(self.rs_parts):
+                if big:
+                    px, py = self.place(f, 1 - fo, lo)
+                    self.rs_send(bank, part, self.z, px, py, self.rs_slot(bank, part, 4 * A + 2), 2, self.near[f])
+
+        def come(part, big, f, l, fo, lo):
+            px, py = self.place(f, fo, lo)
+            self.rs_add(bank, part, self.z, px, py, self.rs_slot(bank, part, 4 * A + 2), out)
+
+        return [go] + [functools.partial(come, *row) for row in self.orders(self.rs_parts) if row[1]]
+
+    def rs_ready(self):
+        for go in (None, pl.semaphore_wait):
+            self.z_credit(go)
+            self.f_credit(go, 4)
+
+    def rs(self, out1, out0):
+        A = self.A
+        sends1, sends0 = self.rs_firsts(1), self.rs_firsts(0)
+        open1, sends1 = sends1[:AHEAD], sends1[AHEAD:]
+        open0, sends0 = sends0[:AHEAD], sends0[AHEAD:]
+        before, after = list(open1), list(open0)
+        small1 = [self.rs_along(1, j, out1, False) for j in range(A)]
+        small0 = [self.rs_along(0, j, out0, False) for j in range(A)]
+        big1 = [self.rs_along(1, j, out1, True) for j in range(A)]
+        big0 = [self.rs_along(0, j, out0, True) for j in range(A)]
+        last1, last0 = self.rs_last(1, out1), self.rs_last(0, out0)
         for j in range(A):
-            z = self.turns[j]
-            for part, big, f, l, fo, lo in info:
-                for w in (1, 0):
-                    fc = fo if w == 0 else 1 - fo
-                    px, py = self.place(f, fc, lo)
-                    self.rs_add(bank, part, z, px, py, z * 2 + fc)
-                    if big:
-                        chain(part, big, f, fc, lo, w, z, None)
-                    elif w == 1:
-                        self.rs_send(bank, part, z, px, py, 2 * A + z, 2, self.near[f])
-                    if big:
-                        yield
-                if not big:
-                    yield
-            for part, big, f, l, fo, lo in info:
-                if not big:
-                    px, py = self.place(f, fo, lo)
-                    self.rs_add(bank, part, z, px, py, 2 * A + z)
-                    chain(part, big, f, fo, lo, 0, z, out if j == A - 1 else None)
-                    yield
-        for part, big, f, l, fo, lo in info:
-            if big:
-                px, py = self.place(f, 1 - fo, lo)
-                self.rs_send(bank, part, self.z, px, py, 4 * A + 2, 2, self.near[f])
-        yield
-        for part, big, f, l, fo, lo in info:
-            if big:
-                px, py = self.place(f, fo, lo)
-                self.rs_add(bank, part, self.z, px, py, 4 * A + 2, out)
-                yield
+            before += zipped(
+                self.rs_across(1, j, sends1), (big1[j] if j < A - 1 else []) + (small1[j - 1] if j else [])
+            )
+        after += [self.rs_ready]
+        after += zipped(self.rs_across(0, 0, sends0), big0[0] + big1[A - 1] + small1[A - 1])
+        after += last1[:1]
+        for j in range(1, A):
+            after += zipped(self.rs_across(0, j, sends0), big0[j] + small0[j - 1])
+            if j == 1:
+                after += last1[1:]
+        after += last0[:1] + small0[A - 1] + last0[1:]
+        return before, after
+
+    def f_credit(self, wait, at):
+        for k, axis in enumerate("xy"):
+            if wait:
+                wait(self.credit.at[at + k], 1)
+            else:
+                pl.semaphore_signal(self.credit.at[at + k], inc=1, device_id=self.near[axis], device_id_type=MESH)
+
+    def z_credit(self, wait):
+        @pl.when(self.has_up)
+        def _():
+            if wait:
+                wait(self.credit.at[3], 1)
+            else:
+                pl.semaphore_signal(self.credit.at[2], inc=1, device_id=self.up, device_id_type=MESH)
+
+        @pl.when(self.has_down)
+        def _():
+            if wait:
+                wait(self.credit.at[2], 1)
+            else:
+                pl.semaphore_signal(self.credit.at[3], inc=1, device_id=self.down, device_id_type=MESH)
 
     def rs_drain(self, bank):
         A = self.A
         base = bank * 2 * A
-        for part, (order, _, rows) in enumerate(self.parts):
+        for part, (order, _, rows) in enumerate(self.rs_parts):
             big = order[0] != "z"
 
             def sent(kind, count):
                 ref = self.wb.at[base : base + count, :, pl.ds(0, rows), :]
-                slot = (bank * len(self.parts) + part) * 4 + kind
+                slot = (bank * len(self.rs_parts) + part) * 4 + kind
                 self.remote(ref, ref, self.rs_s.at[slot], self.rs_r.at[0], self.sib).wait_send()
 
             sent(0, A - 1)
@@ -416,15 +521,32 @@
 
     def give(self, k, halves):
         buf = k % 2
-        for h, value in enumerate(halves(self.rows_of(1 - self.c))):
+        for h, value in enumerate(halves(1 - self.c)):
             self.sb[buf, :, h * TILE : (h + 1) * TILE] = value.astype(BF)
         self.remote(self.sb.at[buf], self.rb.at[buf], self.ex_s.at[k], self.ex_r.at[k], self.sib).start()
-        for h, value in enumerate(halves(self.rows_of(self.c))):
+        for h, value in enumerate(halves(self.c)):
             self.pacc[:, h * TILE : (h + 1) * TILE] = value
 
     def taken(self, k):
         buf = k % 2
         self.remote(self.sb.at[buf], self.rb.at[buf], self.ex_s.at[k], self.ex_r.at[k], self.sib).wait()
+
+
+    def act_at(self, j, m):
+        if self.nt == 1:
+            return (j, m)
+        half = self.nt // 2
+        return (pl.ds(j * self.nt + m * half, half),)
+
+    def act_get(self, j, m):
+        return self.act[self.act_at(j, m)].reshape(self.T, TILE)
+
+    def act_set(self, j, m, value):
+        at = self.act_at(j, m)
+        self.act[at] = value.astype(BF).reshape(self.act.at[at].shape)
+
+    def act_all(self, j):
+        return self.act[pl.ds(j * self.nt, self.nt)].reshape(2 * self.T, TILE)
 
 
     def wcol(self, b):
@@ -460,7 +582,7 @@
         edge = self.pfx_now[0:1, 0:1]
         return jnp.logical_or(key <= query, key.astype(F32) < edge)
 
-    def attend(self, p, qkv, o, lse, masked):
+    def attend(self, p, qkv, o, lse, masked, point):
         T = self.T
         cols = pl.ds(pl.multiple_of(p * PAIR, PAIR), PAIR)
         heads, upper = self.masks()
@@ -480,9 +602,10 @@
                 total = jnp.sum(exponent, axis=0, keepdims=True)
                 lse[p, h : h + 1, rows] = highest + jnp.log(total)
                 mixed.append(dot(values_t, exponent.astype(BF)) * (1.0 / total))
+                point(2 * tile + h)
             o[rows, cols] = jnp.where(upper, mixed[0], mixed[1]).T.astype(BF)
 
-    def attend_back(self, p, qkv, do, lse, masked):
+    def attend_back(self, p, qkv, do, lse, masked, point):
         T = self.T
         cols = pl.ds(pl.multiple_of(p * PAIR, PAIR), PAIR)
         heads, upper = self.masks()
@@ -509,6 +632,7 @@
                 dq.append(dot(keys_t, dscores))
                 dk[h] += dot(dscores, query)
                 dv[h] += dot(probs.astype(BF), grad)
+                point(2 * tile + h)
             self.dqkv[0, rows, cols] = (jnp.where(upper, dq[0], dq[1]) * score_scale).T.astype(BF)
         self.dqkv[1, :, cols] = (jnp.where(heads[0], dk[0], dk[1]) * score_scale).astype(BF)
         self.dqkv[2, :, cols] = jnp.where(heads[0], dv[0], dv[1]).astype(BF)
@@ -536,27 +660,46 @@
             body(own, full)
 
 
-def pump(steps, count):
-    for _ in range(count):
-        next(steps, None)
-
-
-def finish(steps):
-    for _ in steps:
-        pass
-
-
-def in_loop(steps, index, turns, count):
-    for turn in range(turns):
-
-        @pl.when(index == turn)
-        def _():
-            pump(steps, count)
-
-
-def kernel(A, R, T, parts, names, *arrays):
-    s = Layer(A, R, T, parts, dict(zip(names, arrays)))
-    s.land = [getattr(s, f"land{i}") for i in range(len(parts))]
+def zipped(first, second):
+    first, second, steps = list(first), list(second), []
+    while first or second:
+        steps += first[:2] + second[:1]
+        first, second = first[2:], second[1:]
+    return steps
+
+
+class Steps:
+    def __init__(self, steps):
+        self.steps = list(steps)
+
+    def run(self, count):
+        now, self.steps = self.steps[:count], self.steps[count:]
+        for step in now:
+            step()
+
+    def finish(self):
+        self.run(len(self.steps))
+
+    def spread(self, index, turns, points, count=1):
+        total = turns * points * count
+        now, self.steps = self.steps[:total], self.steps[total:]
+
+        def at(point):
+            for turn in range(turns):
+                place = (turn * points + point) * count
+                if now[place : place + count]:
+
+                    @pl.when(index == turn)
+                    def _():
+                        for step in now[place : place + count]:
+                            step()
+
+        return at
+
+
+def kernel(A, R, T, ag_parts, rs_parts, names, *arrays):
+    s = Layer(A, R, T, ag_parts, rs_parts, dict(zip(names, arrays)))
+    s.land = [getattr(s, f"land{i}") for i in range(len(rs_parts))]
     D = s.D
     away = jnp.logical_not(s.kept)
     s.ng[...] = jnp.zeros_like(s.ng)
@@ -594,15 +737,20 @@
         (s.cot, s.cotb, s.cotb),
     ]
 
-    @pl.when(s.kept)
-    def _():
-        for i, (src, dst, _) in enumerate(swaps):
+    def swap(i):
+        src, dst, far = swaps[i]
+
+        @pl.when(s.kept)
+        def _():
             pltpu.make_async_copy(src, dst, s.lc.at[3 + i]).start()
 
-    @pl.when(away)
-    def _():
-        for i, (src, _, dst) in enumerate(swaps):
-            s.remote(src, dst, s.sw_s.at[i], s.sw_r.at[i], s.partner).start()
+        @pl.when(away)
+        def _():
+            s.remote(src, far, s.sw_s.at[i], s.sw_r.at[i], s.partner).start()
+
+    swap(0)
+    swap(1)
+    swap(2)
 
     @pl.when(by_rows)
     def _():
@@ -614,8 +762,8 @@
         half_send.wait_send()
         half_recv.wait_recv()
 
-    gather = s.ag(0)
-    next(gather)
+    gather, ffn = Steps(s.ag(0)), Steps(s.ag(1))
+    gather.run(2)
 
     def swapped(i):
         src, dst, far = swaps[i]
@@ -629,36 +777,34 @@
             s.remote(src, far, s.sw_s.at[i], s.sw_r.at[i], s.partner).wait_send()
             s.remote(src, dst, s.sw_s.at[i], s.sw_r.at[i], s.partner).wait_recv()
 
-    pump(gather, 4)
-    swapped(0)
+    gather.run(14)
+    ffn_copy.wait()
+    ffn.run(1)
+    gather.run(14)
+    ffn.run(1)
+    swap(3)
+    for i in range(3):
+        swapped(i)
     s.share(s.xf, 0)
-    swapped(1)
     s.share(s.mf, 1)
-    swapped(2)
-    pump(gather, 24)
-    swapped(3)
+    gather.finish()
     s.shared(s.xf, 0)
     s.shared(s.mf, 1)
-    ffn_copy.wait()
-    ffn = s.ag(1)
-    next(ffn)
-    finish(gather)
 
     s.project(s.qkv1, 0, s.xf, 0, 3)
-    pump(ffn, 2)
+    ffn.run(2)
     s.project(s.qkv2, 1, s.mf, 5, 2)
-    pump(ffn, 2)
+    ffn.run(2)
 
     @pl.loop(0, TILE // PAIR)
     def _(p):
-        s.attend(p, s.qkv1, s.o1, s.lse1, True)
-        in_loop(ffn, p, TILE // PAIR, 3)
+        s.attend(p, s.qkv1, s.o1, s.lse1, True, ffn.spread(p, TILE // PAIR, 4))
 
     def branch(o, b):
-        return lambda rows: [dot(o[rows, :], s.wrow(b, h)) for h in range(2)]
+        return lambda which: [dot(o[s.rows_of(which), :], s.wrow(b, h)) for h in range(2)]
 
     s.give(0, branch(s.o1, 3))
-    pump(ffn, 1)
+    ffn.run(1)
     s.taken(0)
 
     def first_norm(own, full):
@@ -672,18 +818,17 @@
 
     s.norm_rows(first_norm)
     s.share(s.n1r, 2)
-    pump(ffn, 2)
+    ffn.run(2)
     s.shared(s.n1r, 2)
 
     s.project(s.qkv2, 0, s.n1r, 4, 1)
 
     @pl.loop(0, TILE // PAIR)
     def _(p):
-        s.attend(p, s.qkv2, s.o2, s.lse2, False)
-        in_loop(ffn, p, TILE // PAIR, 3)
+        s.attend(p, s.qkv2, s.o2, s.lse2, False, ffn.spread(p, TILE // PAIR, 4))
 
     s.give(1, branch(s.o2, 7))
-    pump(ffn, 1)
+    ffn.run(1)
     s.taken(1)
 
     def second_norm(own, full):
@@ -697,9 +842,10 @@
 
     s.norm_rows(second_norm)
     s.share(s.n2r, 3)
-    pump(ffn, 2)
+    ffn.run(2)
     s.shared(s.n2r, 3)
-    finish(ffn)
+    ffn.finish()
+    swapped(3)
 
     tiles = 2 * A * R // TILE
 
@@ -709,11 +855,11 @@
             rows = slice(m * T, (m + 1) * T)
             pre = dot_nt(s.n2r[rows, :TILE], s.win(j, 0)) + dot_nt(s.n2r[rows, TILE:], s.win(j, 1))
             gate = 1.0 / (1.0 + jnp.exp(-pre))
-            s.act[tiles + j, rows, :] = (pre * gate).astype(BF)
-            s.act[j, rows, :] = (gate * (1.0 + pre * (1.0 - gate))).astype(BF)
-
-    def ffn_out(rows):
-        return [sum(dot(s.act[tiles + j, rows, :], s.wout(j, h)) for j in range(tiles)) for h in range(2)]
+            s.act_set(tiles + j, m, pre * gate)
+            s.act_set(j, m, gate * (1.0 + pre * (1.0 - gate)))
+
+    def ffn_out(which):
+        return [sum(dot(s.act_get(tiles + j, which), s.wout(j, h)) for j in range(tiles)) for h in range(2)]
 
     s.give(2, ffn_out)
     s.taken(2)
@@ -746,16 +892,16 @@
         for m in range(2):
             rows = slice(m * T, (m + 1) * T)
             da = dot_nt(s.ga[rows, :TILE], s.wout(j, 0)) + dot_nt(s.ga[rows, TILE:], s.wout(j, 1))
-            s.act[j, rows, :] = (da * s.act[j, rows, :].astype(F32)).astype(BF)
-
-    def ffn_in(rows):
-        return [sum(dot(s.act[j, rows, :], s.win(j, h)) for j in range(tiles)) for h in range(2)]
+            s.act_set(j, m, da * s.act_get(j, m).astype(F32))
+
+    def ffn_in(which):
+        return [sum(dot(s.act_get(j, which), s.win(j, h)) for j in range(tiles)) for h in range(2)]
 
     s.give(3, ffn_in)
 
     @pl.loop(0, tiles)
     def _(j):
-        hidden, grads = s.act[tiles + j], s.act[j]
+        hidden, grads = s.act_all(tiles + j), s.act_all(j)
         for h in range(2):
             cols = slice(h * TILE, (h + 1) * TILE)
             out_rows = dot_tn(hidden, s.ga[:, cols]).astype(BF)
@@ -763,9 +909,9 @@
             in_rows = dot_tn(grads, s.n2r[:, cols]).astype(BF)
             s.wb[pl.ds(2 * A + j * s.nt, s.nt), h] = in_rows.reshape(s.nt, 2 * R, TILE)
 
-    for j in range(A):
-        s.rs_first(1, s.turns[j])
-    spread = s.rs(1, s.dffn)
+    s.f_credit(None, 0)
+    spread, rest = (Steps(steps) for steps in s.rs(s.dffn, s.fin))
+    spread.run(AHEAD)
     s.taken(3)
 
     def second_back(own, full):
@@ -776,7 +922,7 @@
 
     s.norm_rows(second_back)
     s.share(s.gb, 5)
-    pump(spread, 2)
+    spread.run(3)
     s.shared(s.gb, 5)
 
     def mixed_back(grad, o, b):
@@ -800,7 +946,8 @@
             else:
                 s.wb[b, h] = terms
 
-    def spread_back(rows, blocks):
+    def spread_back(which, blocks):
+        rows = s.rows_of(which)
         halves = []
         for h in range(2):
             total = 0.0
@@ -810,15 +957,14 @@
         return halves
 
     mixed_back(s.gb, s.o2, 7)
-    pump(spread, 2)
+    spread.run(3)
 
     @pl.loop(0, TILE // PAIR)
     def _(p):
-        s.attend_back(p, s.qkv2, s.do, s.lse2, False)
-        in_loop(spread, p, TILE // PAIR, 3)
-
-    s.give(4, lambda rows: spread_back(rows, [(5, 1), (6, 2)]))
-    pump(spread, 1)
+        s.attend_back(p, s.qkv2, s.do, s.lse2, False, spread.spread(p, TILE // PAIR, 4))
+
+    s.give(4, lambda which: spread_back(which, [(5, 1), (6, 2)]))
+    spread.run(2)
     s.taken(4)
 
     def memory_rows(own, full):
@@ -828,12 +974,12 @@
 
     s.norm_rows(memory_rows)
     send_back(1)
-    s.give(5, lambda rows: spread_back(rows, [(4, 0)]))
-    pump(spread, 1)
+    s.give(5, lambda which: spread_back(which, [(4, 0)]))
+    spread.run(2)
     weight_terms(4, s.n1r, s.dqkv[0])
     weight_terms(5, s.mf, s.dqkv[1])
     weight_terms(6, s.mf, s.dqkv[2])
-    pump(spread, 1)
+    spread.run(2)
     s.taken(5)
 
     def first_back(own, full):
@@ -844,7 +990,7 @@
 
     s.norm_rows(first_back)
     s.share(s.ga, 6)
-    pump(spread, 2)
+    spread.run(3)
     s.shared(s.ga, 6)
 
     def norm_sum():
@@ -882,23 +1028,22 @@
     next(sums)
 
     mixed_back(s.ga, s.o1, 3)
-    pump(spread, 2)
+    spread.run(3)
     next(sums)
 
     @pl.loop(0, TILE // PAIR)
     def _(p):
-        s.attend_back(p, s.qkv1, s.do, s.lse1, True)
-        in_loop(spread, p, TILE // PAIR, 4)
+        s.attend_back(p, s.qkv1, s.do, s.lse1, True, spread.spread(p, TILE // PAIR, 4))
 
     next(sums)
-    s.give(6, lambda rows: spread_back(rows, [(0, 0), (1, 1), (2, 2)]))
+    s.give(6, lambda which: spread_back(which, [(0, 0), (1, 1), (2, 2)]))
     next(sums)
 
     @pl.loop(0, 3)
     def _(k):
         weight_terms(k, s.xf, s.dqkv[k])
 
-    finish(sums)
+    next(sums, None)
     s.taken(6)
 
     def token_rows(own, full):
@@ -908,32 +1053,9 @@
 
     s.norm_rows(token_rows)
     send_back(2)
-    finish(spread)
-
-    for k, device in enumerate((s.near["x"], s.near["y"])):
-        pl.semaphore_signal(s.credit.at[k], inc=1, device_id=device, device_id_type=MESH)
-
-    @pl.when(s.has_up)
-    def _():
-        pl.semaphore_signal(s.credit.at[2], inc=1, device_id=s.up, device_id_type=MESH)
-
-    @pl.when(s.has_down)
-    def _():
-        pl.semaphore_signal(s.credit.at[3], inc=1, device_id=s.down, device_id_type=MESH)
-
-    pl.semaphore_wait(s.credit.at[0], 1)
-    pl.semaphore_wait(s.credit.at[1], 1)
-
-    @pl.when(s.has_down)
-    def _():
-        pl.semaphore_wait(s.credit.at[2], 1)
-
-    @pl.when(s.has_up)
-    def _():
-        pl.semaphore_wait(s.credit.at[3], 1)
-
-    for j in range(A):
-        s.rs_first(0, s.turns[j])
+    spread.finish()
+    s.f_credit(pl.semaphore_wait, 0)
+    rest.run(AHEAD)
 
     @pl.when(away)
     def _():
@@ -945,7 +1067,7 @@
                 own = pl.ds(pl.multiple_of(i * LN_ROWS, LN_ROWS), LN_ROWS)
                 dst[own, :] = s.orb[k, own, :].astype(F32)
 
-    finish(s.rs(0, s.fin))
+    rest.finish()
 
     tail_send = s.remote(s.fin.at[1 - s.c], s.dattn.at[s.c], s.misc_s.at[1], s.misc_r.at[1], s.sib)
     tail_recv = s.remote(s.fin.at[1 - s.c], s.dattn.at[1 - s.c], s.misc_s.at[1], s.misc_r.at[1], s.sib)
@@ -968,7 +1090,7 @@
 def on_device(A, tokens, memory, attn_bank, ffn_bank, norm_params, prefix, cotangent):
     T, D = tokens.shape
     R = attn_bank.shape[0]
-    parts = cut(R)
+    ag_parts, rs_parts = cut(R, GATHER), cut(R, SCATTER)
     groups = D // (4 * R)
     tiles = 2 * A * R // TILE
 
@@ -984,8 +1106,7 @@
     if groups > 1:
         attn_piece = jnp.where(by_rows, attn_piece, by_core(attn_bank))
     pfx = jnp.broadcast_to(prefix.astype(F32)[0], (8, 128))
-    np_ = len(parts)
-    slots = sum(slots_of(order, A) for order, _, _ in parts)
+    slots = sum(slots_of(order, A) + 3 for order, _, _ in rs_parts)
 
     inputs = dict(
         tokens=tokens,
@@ -1012,7 +1133,7 @@
         ga=low(2 * T, D),
         gb=low(2 * T, D),
         cotb=low(T, D),
-        act=low(2 * tiles, 2 * T, TILE),
+        act=low(2 * A, 2, R, TILE),
         qkv1=low(3, 2 * T, TILE),
         qkv2=low(3, 2 * T, TILE),
         dqkv=low(3, 2 * T, TILE),
@@ -1040,10 +1161,10 @@
         misc_r=dma(2),
         sw_s=dma(4),
         sw_r=dma(4),
-        ag_s=dma(2 * np_ * 4),
-        ag_r=dma(2 * np_ * 4 * A),
-        rs_s=dma(2 * np_ * 4),
-        rs_r=dma(slots),
+        ag_s=dma(2 * len(ag_parts) * 4),
+        ag_r=dma(2 * len(ag_parts) * 4 * A),
+        rs_s=dma(2 * len(rs_parts) * 4),
+        rs_r=dma(3 * slots),
         cg_s=dma(7),
         cg_r=dma(7),
         ex_s=dma(7),
@@ -1052,13 +1173,13 @@
         ob_r=dma(3),
         nm_s=dma(3 + A),
         nm_r=dma(3 + A),
-        credit=pltpu.SemaphoreType.REGULAR((4,)),
+        credit=pltpu.SemaphoreType.REGULAR((6,)),
     )
-    for i, (order, _, rows) in enumerate(parts):
-        scratch[f"land{i}"] = low(slots_of(order, A), 2, rows, TILE)
+    for i, (order, _, rows) in enumerate(rs_parts):
+        scratch[f"land{i}"] = low(slots_of(order, A) + (3 if order[0] != "z" else 1), 2, rows, TILE)
     names = list(inputs) + list(outputs) + list(scratch)
     out, dtok, dmem, dattn, dffn, dnorm = pl.pallas_call(
-        functools.partial(kernel, A, R, T, parts, names),
+        functools.partial(kernel, A, R, T, ag_parts, rs_parts, names),
         out_shape=[jax.ShapeDtypeStruct(shape, F32) for shape in outputs.values()],
         in_specs=[pl.BlockSpec(memory_space=pltpu.VMEM if n in in_vmem else pl.ANY) for n in inputs],
         out_specs=[pl.BlockSpec(memory_space=pltpu.VMEM)] * len(outputs),

time: 430 us -> 346 us (0.80)
  Pallas kernels: 410 us -> 326 us
    pallas_call x1, Pallas kernels: 410 us -> 326 us  [on_device(): pl.pallas_call(functools.partial(kernel, A, R, T, ag_parts, rs_parts, nam...]
where the time goes in v2:
time: 346 us; the launch traced here: 341 us
  Pallas kernels  326 us (94%)
  local copies, waits for them, and re-layouts  13.4 us (4%)
    pallas_call x1, Pallas kernels, on_device(): pl.pallas_call(functools.partial(kernel, A, R, T, ag_parts, rs_parts, nam...  326 us
    unnamed x20, local copies, waits for them, and re-layouts  8.89 us

profile of v2, /device:TPU:0, one launch (start us, length us, event | category | flops | bytes accessed | tf_op | source)
XLA Modules:
  0.0 341.0 jit_solution(10830715503694448522)
XLA Ops:
  1.3 0.6 broadcast_in_dim.3.arrays_3_
  1.9 1.2 copy.13
  3.1 0.0 copy-start.4
  3.1 1.0 copy.14
  4.1 0.0 copy-done.4
  4.2 0.2 copy.15
  4.4 1.0 copy.16
  5.4 325.8 %layer.1 = (f32[256,1024]{1,0:T(8,128)}, f32[256,1024]{1,0:T(8,128)}, f32[256,1024]{1,0:T(8,128)}, f32[2,256,512]{2,1,0:T(8,128)}, f32[2,256,512]{2,1,0:T(8,128)}, /*index=5*/f32[6,1024]{1,0:T(8,128)}) custom-call(bf16[256,1024]{1,0:T(8,128)(2,1)} %arrays_0_.1, bf16[256,1024]{1,0:T(8,128)(2,1)} %arrays_1_.1, bf16[256,1024]{1,0:T(8,128)(2,1)} %arrays_2_.1, ...), custom_call_target="tpu_custom_call" | custom-call | tf_op jit(solution)/shard_map/layer/pallas_call | solution.py:1181
  331.2 1.6 copy.17
  332.8 0.0 copy-start.3
  332.8 1.3 copy.19
  334.1 0.0 copy-done.3
  334.1 0.3 copy.18
  334.4 0.0 copy-start.2
  334.4 1.3 copy.20
  335.7 0.0 copy-done.2
  335.8 0.0 copy-start.1
  335.8 1.0 copy.26
  336.7 0.6 copy-done.1
  337.4 0.0 copy-start
  337.4 1.0 copy.27
  338.3 0.6 copy-done
  339.0 0.0 copy-start.5
  339.0 1.0 copy.28
  339.9 0.0 copy-done.5
  339.9 0.6 copy.29
Async XLA Ops:
  3.1 1.0 copy-start.4
  332.8 1.3 copy-start.3
  334.4 1.3 copy-start.2
  335.8 1.6 copy-start.1
  337.4 1.6 copy-start
  339.0 1.0 copy-start.5

commit v3 on v2

--- a/solution.py
+++ b/solution.py
@@ -12,9 +12,18 @@
 TILE = 512
 SUB = 16
 LN_ROWS = 32
+HANDS = 4
 AHEAD = 8
+ACROSS = 11.63
+ALONG = 12.12
+HOP = 9.52
+LAG_BIG = 0.06
+LAG_SMALL = 0.71
+START = 12.51
+FIRST = 3.0
+SECOND = 10.05
 GATHER = (5, 5, 3, 3)
-SCATTER = (5, 5, 3, 3)
+SCATTER = (4, 6, 3, 3)
 
 alpha_scale = 300.0**0.25
 norm_eps = 1e-05
@@ -56,6 +65,10 @@
 
 def slots_of(order, A):
     return 4 * A + 3 if order[0] != "z" else 4 * A + 1
+
+
+def landing(order, A):
+    return slots_of(order, A) + (3 if order[0] != "z" else 1)
 
 
 class Layer:
@@ -125,19 +138,27 @@
             pl.semaphore_wait(bar, 2 + self.A)
 
 
-    def ag_index(self, bank, part, z, x, y):
-        return ((bank * len(self.ag_parts) + part) * 2 * self.A + z * 2 + x) * 2 + y
+    def ag_index(self, bank, part, z, x, y, last):
+        base = (bank * len(self.ag_parts) + part) * (2 * self.A + 1)
+        if last:
+            return base + 2 * self.A
+        return base + z * 2 + (x if self.ag_parts[part][0][2] == "y" else y)
 
     def ag_send(self, bank, part, z, x, y, kind, device):
         ref = self.spot(bank, self.ag_parts[part], z, x, y)
-        slot = (bank * len(self.ag_parts) + part) * 4 + kind
-        self.remote(ref, ref, self.ag_s.at[slot], self.ag_r.at[self.ag_index(bank, part, z, x, y)], device).start()
+        recv = self.ag_r.at[self.ag_index(bank, part, z, x, y, kind == 3)]
+        self.remote(ref, ref, self.ag_s.at[part * 4 + kind], recv, device).start()
 
     def ag_wait(self, bank, part, z, x, y):
         ref = self.spot(bank, self.ag_parts[part], z, x, y)
-        self.remote(
-            ref, ref, self.ag_s.at[0], self.ag_r.at[self.ag_index(bank, part, z, x, y)], self.sib
-        ).wait_recv()
+        recv = self.ag_r.at[self.ag_index(bank, part, z, x, y, False)]
+        self.remote(ref, ref, self.ag_s.at[0], recv, self.sib).wait_recv()
+
+    def ag_last(self, bank, part):
+        _, _, rows = self.ag_parts[part]
+        ref = self.wb.at[0 : 2 * self.A, :, pl.ds(0, rows), :]
+        recv = self.ag_r.at[self.ag_index(bank, part, 0, 0, 0, True)]
+        self.remote(ref, ref, self.ag_s.at[0], recv, self.sib).wait_recv()
 
     def ag(self, bank):
         A = self.A
@@ -208,10 +229,6 @@
                 send(part, f, 1 - fo, lo, z, 3, l)
 
             self.planes_at(d, crossed)
-
-        def end(d, w, part, big, f, l, fo, lo):
-            px, py = self.place(f, w, 1 - lo)
-            self.planes_at(d, lambda z: self.ag_wait(bank, part, z, px, py))
 
         bigs = [row for row in info if row[1]]
         smalls = [row for row in info if not row[1]]
@@ -223,10 +240,7 @@
             steps += [functools.partial(arrive, d, 1, *row) for row in bigs]
             steps += [functools.partial(cross, d - 1, *row) for row in smalls]
         steps += [functools.partial(cross, A - 1, *row) for row in smalls]
-        for d in range(A):
-            for row in info:
-                for w in (0, 1):
-                    steps.append(functools.partial(end, d, w, *row))
+        steps += [functools.partial(self.ag_last, bank, row[0]) for row in info]
         return steps
 
     def planes_at(self, d, act):
@@ -250,18 +264,16 @@
             info.append((part, order[0] != "z", f, l, self.own(f), self.own(l)))
         return info
 
-    def ag_drain(self, bank):
+    def ag_drain(self):
         A = self.A
-        base = bank * 2 * A
+        inner = jnp.logical_and(self.has_up, self.has_down)
         for part, (order, _, rows) in enumerate(self.ag_parts):
             big = order[0] != "z"
 
             def sent(kind, count):
-                ref = self.wb.at[base : base + count, :, pl.ds(0, rows), :]
-                slot = (bank * len(self.ag_parts) + part) * 4 + kind
-                self.remote(ref, ref, self.ag_s.at[slot], self.ag_r.at[0], self.sib).wait_send()
-
-            inner = jnp.logical_and(self.has_up, self.has_down)
+                ref = self.wb.at[0 : 2 * count, :, pl.ds(0, rows), :]
+                self.remote(ref, ref, self.ag_s.at[part * 4 + kind], self.ag_r.at[0], self.sib).wait_send()
+
             for kind in (0, 1) if big else (0,):
 
                 @pl.when(inner)
@@ -290,12 +302,13 @@
         return self.land[part].at[slot]
 
     def rs_index(self, bank, part, slot, first):
-        slots = [slots_of(order, self.A) + 3 for order, _, _ in self.rs_parts]
-        group = 0 if bank == 1 else 1 if first else 2
-        return group * sum(slots) + sum(slots[:part]) + slot
+        room = [landing(order, self.A) for order, _, _ in self.rs_parts]
+        if bank == 0 and first:
+            return sum(room) + part * 2 * self.A + slot
+        return sum(room[:part]) + slot
 
     def rs_send(self, bank, part, z, x, y, slot, kind, device):
-        sem = (bank * len(self.rs_parts) + part) * 4 + kind
+        sem = part * 4 + kind
         self.remote(
             self.spot(bank, self.rs_parts[part], z, x, y),
             self.rs_land(bank, part, slot, kind == 3),
@@ -319,7 +332,7 @@
             if out is None:
                 self.wb[at, h, pl.ds(row, rows), :] = total.astype(BF)
             else:
-                out[h, start : start + rows, :] = total
+                out[start : start + rows, pl.ds(pl.multiple_of(h * TILE, TILE), TILE)] = total
 
     def rs_firsts(self, bank):
         sends = []
@@ -383,7 +396,7 @@
             def _():
                 self.rs_add(bank, part, z, px, py, slot(jnp.where(self.has_down, z, A)), final)
 
-    def rs_across(self, bank, j, sends):
+    def rs_across(self, bank, j, sends, start):
         A, z = self.A, self.turns[j]
 
         def across(w, more, part, big, f, l, fo, lo):
@@ -395,14 +408,18 @@
             if w == 1 and not big:
                 self.rs_send(bank, part, z, px, py, self.rs_slot(bank, part, 2 * A + z), 2, self.near[f])
 
+        rows = [(w, row) for row in self.orders(self.rs_parts) for w in (1, 0)]
         return [
-            functools.partial(across, w, sends.pop(0) if sends else None, *row)
-            for row in self.orders(self.rs_parts)
-            for w in (1, 0)
+            (
+                start + ACROSS * (j + (k + 1) / len(rows)),
+                functools.partial(across, w, sends.pop(0) if sends else None, *row),
+            )
+            for k, (w, row) in enumerate(rows)
         ]
 
-    def rs_along(self, bank, j, out, bigs):
+    def rs_along(self, bank, j, out, first, start):
         A, z = self.A, self.turns[j]
+        at_end = jnp.logical_not(jnp.logical_and(self.has_up, self.has_down))
 
         def along(w, part, big, f, l, fo, lo):
             if big:
@@ -412,12 +429,26 @@
                 self.rs_add(bank, part, z, px, py, self.rs_slot(bank, part, 2 * A + z))
                 self.chain(bank, part, big, f, fo, lo, 0, z, out if j == A - 1 else None)
 
-        return [
-            functools.partial(along, w, *row)
-            for row in self.orders(self.rs_parts)
-            if row[1] == bigs
-            for w in ((1, 0) if bigs else (0,))
-        ]
+        def only(role, step):
+            @pl.when(role)
+            def _():
+                step()
+
+        orders = self.orders(self.rs_parts)
+        rows = [(w, row) for row in orders if row[1] for w in (1, 0)] + [(0, row) for row in orders if not row[1]]
+        plane = min(j, A - 2 + (0.0 if j == A - 1 else -0.5))
+        steps = []
+        for k, (w, row) in enumerate(rows):
+            step = functools.partial(along, w, *row)
+            inner = start + ALONG * (plane + (k + 1) / len(rows)) + HOP
+            lag = LAG_BIG if row[1] else LAG_SMALL
+            end = first + ACROSS * (j + lag + (k + 1) / len(rows))
+            if j == A - 1:
+                steps.append((max(inner, end), step))
+            else:
+                steps.append((max(inner, end), functools.partial(only, jnp.logical_not(at_end), step)))
+                steps.append((end, functools.partial(only, at_end, step)))
+        return steps
 
     def rs_last(self, bank, out):
         A = self.A
@@ -441,28 +472,19 @@
 
     def rs(self, out1, out0):
         A = self.A
-        sends1, sends0 = self.rs_firsts(1), self.rs_firsts(0)
-        open1, sends1 = sends1[:AHEAD], sends1[AHEAD:]
-        open0, sends0 = sends0[:AHEAD], sends0[AHEAD:]
-        before, after = list(open1), list(open0)
-        small1 = [self.rs_along(1, j, out1, False) for j in range(A)]
-        small0 = [self.rs_along(0, j, out0, False) for j in range(A)]
-        big1 = [self.rs_along(1, j, out1, True) for j in range(A)]
-        big0 = [self.rs_along(0, j, out0, True) for j in range(A)]
-        last1, last0 = self.rs_last(1, out1), self.rs_last(0, out0)
-        for j in range(A):
-            before += zipped(
-                self.rs_across(1, j, sends1), (big1[j] if j < A - 1 else []) + (small1[j - 1] if j else [])
-            )
-        after += [self.rs_ready]
-        after += zipped(self.rs_across(0, 0, sends0), big0[0] + big1[A - 1] + small1[A - 1])
-        after += last1[:1]
-        for j in range(1, A):
-            after += zipped(self.rs_across(0, j, sends0), big0[j] + small0[j - 1])
-            if j == 1:
-                after += last1[1:]
-        after += last0[:1] + small0[A - 1] + last0[1:]
-        return before, after
+        due = []
+        for bank, out, first, start in ((1, out1, 0.0, START), (0, out0, ACROSS * A + FIRST, ALONG * (A - 1) + SECOND)):
+            sends = self.rs_firsts(bank)
+            due += [(first if bank else first - FIRST / 4, step) for step in sends[:AHEAD]]
+            sends = sends[AHEAD:]
+            for j in range(A):
+                due += self.rs_across(bank, j, sends, first)
+                due += self.rs_along(bank, j, out, first, start)
+            done = start + ALONG * (A - 1) + HOP
+            go, *come = self.rs_last(bank, out)
+            due += [(done, go)] + [(done + 2 * HOP, step) for step in come]
+        due.append((ACROSS * A + FIRST / 2, self.rs_ready))
+        return sorted(due, key=lambda step: step[0])
 
     def f_credit(self, wait, at):
         for k, axis in enumerate("xy"):
@@ -486,16 +508,14 @@
             else:
                 pl.semaphore_signal(self.credit.at[3], inc=1, device_id=self.down, device_id_type=MESH)
 
-    def rs_drain(self, bank):
+    def rs_drain(self):
         A = self.A
-        base = bank * 2 * A
         for part, (order, _, rows) in enumerate(self.rs_parts):
             big = order[0] != "z"
 
             def sent(kind, count):
-                ref = self.wb.at[base : base + count, :, pl.ds(0, rows), :]
-                slot = (bank * len(self.rs_parts) + part) * 4 + kind
-                self.remote(ref, ref, self.rs_s.at[slot], self.rs_r.at[0], self.sib).wait_send()
+                ref = self.wb.at[0 : 2 * count, :, pl.ds(0, rows), :]
+                self.remote(ref, ref, self.rs_s.at[part * 4 + kind], self.rs_r.at[0], self.sib).wait_send()
 
             sent(0, A - 1)
             if big:
@@ -660,17 +680,9 @@
             body(own, full)
 
 
-def zipped(first, second):
-    first, second, steps = list(first), list(second), []
-    while first or second:
-        steps += first[:2] + second[:1]
-        first, second = first[2:], second[1:]
-    return steps
-
-
 class Steps:
-    def __init__(self, steps):
-        self.steps = list(steps)
+    def __init__(self, steps, limit=1e9):
+        self.steps, self.limit = list(steps), limit
 
     def run(self, count):
         now, self.steps = self.steps[:count], self.steps[count:]
@@ -679,6 +691,29 @@
 
     def finish(self):
         self.run(len(self.steps))
+
+    def until(self, time):
+        while self.steps and self.steps[0][0] <= min(time, self.limit):
+            self.steps.pop(0)[1]()
+
+    def timed(self, index, turns, points, start, length):
+        groups = []
+        for place in range(turns * points):
+            time, group = start + length * (place + 1) / (turns * points), []
+            while self.steps and self.steps[0][0] <= min(time, self.limit):
+                group.append(self.steps.pop(0)[1])
+            groups.append(group)
+
+        def at(point):
+            for turn in range(turns):
+                if groups[turn * points + point]:
+
+                    @pl.when(index == turn)
+                    def _():
+                        for step in groups[turn * points + point]:
+                            step()
+
+        return at
 
     def spread(self, index, turns, points, count=1):
         total = turns * points * count
@@ -703,25 +738,33 @@
     D = s.D
     away = jnp.logical_not(s.kept)
     s.ng[...] = jnp.zeros_like(s.ng)
+    s.pfx_own[...] = jnp.full(s.pfx_own.shape, s.pfx[0], jnp.int32).astype(F32)
     s.barrier()
 
     block = s.zx // s.nzx
     by_rows = jnp.logical_or(block == 3, block == 7)
     mine = pl.ds(pl.multiple_of(s.y * R, SUB), R)
-    ffn_copy = pltpu.make_async_copy(s.ffn_piece, s.wb.at[2 * A + s.zx, :, mine, :], s.lc.at[0])
-    ffn_copy.start()
-    rows_copy = pltpu.make_async_copy(s.attn_piece, s.wb.at[s.zx, :, mine, :], s.lc.at[1])
-    half_copy = pltpu.make_async_copy(s.attn_piece.at[s.c], s.wb.at[s.zx, s.c, mine, :], s.lc.at[2])
+    half = [pl.ds(pl.multiple_of(h * TILE, TILE), TILE) for h in (0, 1, s.c, 1 - s.c)]
+    ffn_copies = [
+        pltpu.make_async_copy(s.ffn_rows.at[:, half[h]], s.wb.at[2 * A + s.zx, h, mine, :], s.lc.at[h]) for h in (0, 1)
+    ]
+    rows_copies = [
+        pltpu.make_async_copy(s.attn_rows.at[:, half[h]], s.wb.at[s.zx, h, mine, :], s.lc.at[2 + h]) for h in (0, 1)
+    ]
+    half_copy = pltpu.make_async_copy(s.attn_rows.at[:, half[2]], s.wb.at[s.zx, s.c, mine, :], s.lc.at[2])
     half_send = s.remote(
-        s.attn_piece.at[1 - s.c], s.wb.at[s.zx, s.c, mine, :], s.misc_s.at[0], s.misc_r.at[0], s.sib
+        s.attn_rows.at[:, half[3]], s.wb.at[s.zx, s.c, mine, :], s.misc_s.at[0], s.misc_r.at[0], s.sib
     )
     half_recv = s.remote(
-        s.attn_piece.at[1 - s.c], s.wb.at[s.zx, 1 - s.c, mine, :], s.misc_s.at[0], s.misc_r.at[0], s.sib
+        s.attn_rows.at[:, half[3]], s.wb.at[s.zx, 1 - s.c, mine, :], s.misc_s.at[0], s.misc_r.at[0], s.sib
     )
+    for copy in ffn_copies:
+        copy.start()
 
     @pl.when(by_rows)
     def _():
-        rows_copy.start()
+        for copy in rows_copies:
+            copy.start()
 
     @pl.when(jnp.logical_not(by_rows))
     def _():
@@ -733,7 +776,7 @@
     swaps = [
         (s.tokens, s.xf.at[here, :], s.xf.at[there, :]),
         (s.memory, s.mf.at[here, :], s.mf.at[there, :]),
-        (s.pfx, s.pfx_now, s.pfx_now),
+        (s.pfx_own, s.pfx_now, s.pfx_now),
         (s.cot, s.cotb, s.cotb),
     ]
 
@@ -742,7 +785,7 @@
 
         @pl.when(s.kept)
         def _():
-            pltpu.make_async_copy(src, dst, s.lc.at[3 + i]).start()
+            pltpu.make_async_copy(src, dst, s.lc.at[4 + i]).start()
 
         @pl.when(away)
         def _():
@@ -754,7 +797,8 @@
 
     @pl.when(by_rows)
     def _():
-        rows_copy.wait()
+        for copy in rows_copies:
+            copy.wait()
 
     @pl.when(jnp.logical_not(by_rows))
     def _():
@@ -770,7 +814,7 @@
 
         @pl.when(s.kept)
         def _():
-            pltpu.make_async_copy(src, dst, s.lc.at[3 + i]).wait()
+            pltpu.make_async_copy(src, dst, s.lc.at[4 + i]).wait()
 
         @pl.when(away)
         def _():
@@ -778,7 +822,8 @@
             s.remote(src, dst, s.sw_s.at[i], s.sw_r.at[i], s.partner).wait_recv()
 
     gather.run(14)
-    ffn_copy.wait()
+    for copy in ffn_copies:
+        copy.wait()
     ffn.run(1)
     gather.run(14)
     ffn.run(1)
@@ -883,8 +928,7 @@
             s.remote(s.osb.at[k], s.orb.at[k], s.ob_s.at[k], s.ob_r.at[k], s.partner).start()
 
     send_back(0)
-    s.ag_drain(0)
-    s.ag_drain(1)
+    s.ag_drain()
     s.shared(s.ga, 4)
 
     @pl.loop(0, tiles)
@@ -910,8 +954,8 @@
             s.wb[pl.ds(2 * A + j * s.nt, s.nt), h] = in_rows.reshape(s.nt, 2 * R, TILE)
 
     s.f_credit(None, 0)
-    spread, rest = (Steps(steps) for steps in s.rs(s.dffn, s.fin))
-    spread.run(AHEAD)
+    spread = Steps(s.rs(s.dffn, s.fin), ACROSS * A)
+    spread.until(0.0)
     s.taken(3)
 
     def second_back(own, full):
@@ -922,7 +966,7 @@
 
     s.norm_rows(second_back)
     s.share(s.gb, 5)
-    spread.run(3)
+    spread.until(3.0)
     s.shared(s.gb, 5)
 
     def mixed_back(grad, o, b):
@@ -957,14 +1001,14 @@
         return halves
 
     mixed_back(s.gb, s.o2, 7)
-    spread.run(3)
+    spread.until(5.0)
 
     @pl.loop(0, TILE // PAIR)
     def _(p):
-        s.attend_back(p, s.qkv2, s.do, s.lse2, False, spread.spread(p, TILE // PAIR, 4))
+        s.attend_back(p, s.qkv2, s.do, s.lse2, False, spread.timed(p, TILE // PAIR, 4, 5.0, 8.0))
 
     s.give(4, lambda which: spread_back(which, [(5, 1), (6, 2)]))
-    spread.run(2)
+    spread.until(15.0)
     s.taken(4)
 
     def memory_rows(own, full):
@@ -975,11 +1019,11 @@
     s.norm_rows(memory_rows)
     send_back(1)
     s.give(5, lambda which: spread_back(which, [(4, 0)]))
-    spread.run(2)
+    spread.until(18.0)
     weight_terms(4, s.n1r, s.dqkv[0])
     weight_terms(5, s.mf, s.dqkv[1])
     weight_terms(6, s.mf, s.dqkv[2])
-    spread.run(2)
+    spread.until(21.0)
     s.taken(5)
 
     def first_back(own, full):
@@ -990,7 +1034,7 @@
 
     s.norm_rows(first_back)
     s.share(s.ga, 6)
-    spread.run(3)
+    spread.until(24.0)
     s.shared(s.ga, 6)
 
     def norm_sum():
@@ -1028,12 +1072,12 @@
     next(sums)
 
     mixed_back(s.ga, s.o1, 3)
-    spread.run(3)
+    spread.until(27.0)
     next(sums)
 
     @pl.loop(0, TILE // PAIR)
     def _(p):
-        s.attend_back(p, s.qkv1, s.do, s.lse1, True, spread.spread(p, TILE // PAIR, 4))
+        s.attend_back(p, s.qkv1, s.do, s.lse1, True, spread.timed(p, TILE // PAIR, 4, 27.0, 9.0))
 
     next(sums)
     s.give(6, lambda which: spread_back(which, [(0, 0), (1, 1), (2, 2)]))
@@ -1053,9 +1097,10 @@
 
     s.norm_rows(token_rows)
     send_back(2)
-    spread.finish()
+    spread.until(1e9)
     s.f_credit(pl.semaphore_wait, 0)
-    rest.run(AHEAD)
+    spread.limit = 1e9
+    spread.until(ACROSS * A + 4.0)
 
     @pl.when(away)
     def _():
@@ -1067,10 +1112,14 @@
                 own = pl.ds(pl.multiple_of(i * LN_ROWS, LN_ROWS), LN_ROWS)
                 dst[own, :] = s.orb[k, own, :].astype(F32)
 
-    rest.finish()
-
-    tail_send = s.remote(s.fin.at[1 - s.c], s.dattn.at[s.c], s.misc_s.at[1], s.misc_r.at[1], s.sib)
-    tail_recv = s.remote(s.fin.at[1 - s.c], s.dattn.at[1 - s.c], s.misc_s.at[1], s.misc_r.at[1], s.sib)
+    spread.until(1e9)
+
+    tail_send = s.remote(
+        s.fin.at[:, half[3]], s.dattn.at[:, half[2]], s.misc_s.at[1], s.misc_r.at[1], s.sib
+    )
+    tail_recv = s.remote(
+        s.fin.at[:, half[3]], s.dattn.at[:, half[3]], s.misc_s.at[1], s.misc_r.at[1], s.sib
+    )
 
     @pl.when(by_rows)
     def _():
@@ -1079,12 +1128,25 @@
     @pl.when(jnp.logical_not(by_rows))
     def _():
         tail_send.start()
-        s.dattn[s.c] = s.fin[s.c]
+        s.dattn[:, half[2]] = s.fin[:, half[2]]
         tail_send.wait_send()
         tail_recv.wait_recv()
 
-    s.rs_drain(1)
-    s.rs_drain(0)
+    s.rs_drain()
+
+
+def hand_on(*refs):
+    for src, dst in zip(refs[: len(refs) // 2], refs[len(refs) // 2 :]):
+        dst[...] = src[...]
+
+
+def hand_specs(outputs):
+    return [
+        pl.BlockSpec(shape, lambda i: (0, 0))
+        if shape[0] % (8 * HANDS)
+        else pl.BlockSpec((shape[0] // HANDS, shape[1]), lambda i: (i, 0))
+        for shape in outputs.values()
+    ]
 
 
 def on_device(A, tokens, memory, attn_bank, ffn_bank, norm_params, prefix, cotangent):
@@ -1094,32 +1156,26 @@
     groups = D // (4 * R)
     tiles = 2 * A * R // TILE
 
-    def by_half(shard):
-        return shard.reshape(R, 2, TILE).transpose(1, 0, 2)
-
-    def by_core(shard):
-        return shard.reshape(R, groups, 2, 2 * R).transpose(2, 0, 1, 3).reshape(2, R, TILE)
-
     block = (lax.axis_index("dp") // 2) // groups
     by_rows = jnp.logical_or(block == 3, block == 7)
-    attn_piece = by_half(attn_bank)
+    attn_rows = attn_bank
     if groups > 1:
-        attn_piece = jnp.where(by_rows, attn_piece, by_core(attn_bank))
-    pfx = jnp.broadcast_to(prefix.astype(F32)[0], (8, 128))
-    slots = sum(slots_of(order, A) + 3 for order, _, _ in rs_parts)
+        by_core = attn_bank.reshape(R, groups, 2, 2 * R).transpose(0, 2, 1, 3).reshape(R, D)
+        attn_rows = jnp.where(by_rows, attn_bank, by_core)
+    slots = sum(landing(order, A) for order, _, _ in rs_parts)
 
     inputs = dict(
         tokens=tokens,
         memory=memory,
         cot=cotangent,
-        pfx=pfx,
-        attn_piece=attn_piece,
-        ffn_piece=by_half(ffn_bank),
+        pfx=prefix,
+        attn_rows=attn_rows,
+        ffn_rows=ffn_bank,
         norms=norm_params,
     )
-    in_vmem = ("pfx", "norms")
+    where = dict(pfx=pltpu.SMEM, norms=pltpu.VMEM)
     outputs = dict(
-        out=(T, D), dtok=(T, D), dmem=(T, D), dattn=(2, R, TILE), dffn=(2, R, TILE), dnorm=(6, D)
+        out=(T, D), dtok=(T, D), dmem=(T, D), dattn=(R, D), dffn=(R, D), dnorm=(6, D)
     )
     wide = lambda *shape: pltpu.VMEM(shape, F32)
     low = lambda *shape: pltpu.VMEM(shape, BF)
@@ -1146,7 +1202,8 @@
         orb=low(3, T, D),
         nbuf=wide(T, D),
         pacc=wide(T, D),
-        fin=wide(2, R, TILE),
+        fin=wide(R, D),
+        pfx_own=wide(8, 128),
         pfx_now=wide(8, 128),
         lse1=wide(TILE // PAIR, 8, 2 * T),
         lse2=wide(TILE // PAIR, 8, 2 * T),
@@ -1156,15 +1213,15 @@
         ngs=wide(3, 8, D),
         ngr=wide(3, 8, D),
         ngz=wide(A, 8, D),
-        lc=dma(7),
+        lc=dma(8),
         misc_s=dma(2),
         misc_r=dma(2),
         sw_s=dma(4),
         sw_r=dma(4),
-        ag_s=dma(2 * len(ag_parts) * 4),
-        ag_r=dma(2 * len(ag_parts) * 4 * A),
-        rs_s=dma(2 * len(rs_parts) * 4),
-        rs_r=dma(3 * slots),
+        ag_s=dma(len(ag_parts) * 4),
+        ag_r=dma(2 * len(ag_parts) * (2 * A + 1)),
+        rs_s=dma(len(rs_parts) * 4),
+        rs_r=dma(slots + len(rs_parts) * 2 * A),
         cg_s=dma(7),
         cg_r=dma(7),
         ex_s=dma(7),
@@ -1176,12 +1233,12 @@
         credit=pltpu.SemaphoreType.REGULAR((6,)),
     )
     for i, (order, _, rows) in enumerate(rs_parts):
-        scratch[f"land{i}"] = low(slots_of(order, A) + (3 if order[0] != "z" else 1), 2, rows, TILE)
+        scratch[f"land{i}"] = low(landing(order, A), 2, rows, TILE)
     names = list(inputs) + list(outputs) + list(scratch)
-    out, dtok, dmem, dattn, dffn, dnorm = pl.pallas_call(
+    results = pl.pallas_call(
         functools.partial(kernel, A, R, T, ag_parts, rs_parts, names),
         out_shape=[jax.ShapeDtypeStruct(shape, F32) for shape in outputs.values()],
-        in_specs=[pl.BlockSpec(memory_space=pltpu.VMEM if n in in_vmem else pl.ANY) for n in inputs],
+        in_specs=[pl.BlockSpec(memory_space=where.get(n, pl.ANY)) for n in inputs],
         out_specs=[pl.BlockSpec(memory_space=pltpu.VMEM)] * len(outputs),
         scratch_shapes=list(scratch.values()),
         compiler_params=pltpu.CompilerParams(
@@ -1190,16 +1247,19 @@
         name="layer",
     )(*inputs.values())
 
-    def half_back(pieces):
-        return pieces.transpose(1, 0, 2).reshape(R, D)
-
-    def core_back(pieces):
-        return pieces.reshape(2, R, groups, 2 * R).transpose(1, 2, 0, 3).reshape(R, D)
-
-    attn_rows = half_back(dattn)
+    results = pl.pallas_call(
+        hand_on,
+        grid=(HANDS,),
+        out_shape=[jax.ShapeDtypeStruct(shape, F32) for shape in outputs.values()],
+        in_specs=hand_specs(outputs),
+        out_specs=hand_specs(outputs),
+        name="hand_on",
+    )(*results)
+    out, dtok, dmem, dattn, dffn, dnorm = results
     if groups > 1:
-        attn_rows = jnp.where(by_rows, attn_rows, core_back(dattn))
-    return (out, dtok, dmem, attn_rows, half_back(dffn), dnorm)
+        by_core = dattn.reshape(R, 2, groups, 2 * R).transpose(0, 2, 1, 3).reshape(R, D)
+        dattn = jnp.where(by_rows, dattn, by_core)
+    return (out, dtok, dmem, dattn, dffn, dnorm)
 
 
 def solution(mesh):

time: 346 us -> 328 us (0.948)
  the two profiles are of different devices: /device:TPU:0 before, /device:TPU:19 now
where the time goes in v3:
time: 328 us; the launch traced here: 323 us
  Pallas kernels  322 us (98%)
    pallas_call x1, Pallas kernels, on_device(): pl.pallas_call(functools.partial(kernel, A, R, T, ag_parts, rs_parts, nam...  317 us

profile of v3, /device:TPU:19, one launch (start us, length us, event | category | flops | bytes accessed | tf_op | source)
XLA Modules:
  0.0 323.4 jit_solution(5430555233424038798)
XLA Ops:
  1.3 316.5 %layer.1 = (f32[256,1024]{1,0:T(8,128)}, f32[256,1024]{1,0:T(8,128)}, f32[256,1024]{1,0:T(8,128)}, f32[256,1024]{1,0:T(8,128)}, f32[256,1024]{1,0:T(8,128)}, /*index=5*/f32[6,1024]{1,0:T(8,128)}) custom-call(bf16[256,1024]{1,0:T(8,128)(2,1)} %arrays_0_.1, bf16[256,1024]{1,0:T(8,128)(2,1)} %arrays_1_.1, bf16[256,1024]{1,0:T(8,128)(2,1)} %arrays_2_.1, ...), custom_call_target="tpu_custom_call" | custom-call | tf_op jit(solution)/shard_map/layer/pallas_call | solution.py:1238
  317.8 5.3 %hand_on.1 = (f32[256,1024]{1,0:T(8,128)}, f32[256,1024]{1,0:T(8,128)}, f32[256,1024]{1,0:T(8,128)}, f32[256,1024]{1,0:T(8,128)}, f32[256,1024]{1,0:T(8,128)}, /*index=5*/f32[6,1024]{1,0:T(8,128)}) custom-call(f32[256,1024]{1,0:T(8,128)} %get-tuple-element.12.refs_0_, f32[256,1024]{1,0:T(8,128)} %get-tuple-element.13.refs_1_, ...), custom_call_target="tpu_custom_call" | custom-call | tf_op jit(solution)/shard_map/hand_on/pallas_call | solution.py:1250

commit v4 on v3

--- a/solution.py
+++ b/solution.py
@@ -22,7 +22,19 @@
 START = 12.51
 FIRST = 3.0
 SECOND = 10.05
-GATHER = (5, 5, 3, 3)
+MIDDLE = 85.0
+EARLY = 5.87
+COME = 10.6
+PLANE = 13.85
+STEP = 1.58
+BESIDE = 9.75
+CROSS = 10.02
+SECOND_BANK = 51.38
+SWAPS = 35.59
+LATE_SWAP = 64.42
+GATHERED = 66.95
+RATE = 1.06
+GATHER = (5, 6, 2, 3)
 SCATTER = (4, 6, 3, 3)
 
 alpha_scale = 300.0**0.25
@@ -160,9 +172,9 @@
         recv = self.ag_r.at[self.ag_index(bank, part, 0, 0, 0, True)]
         self.remote(ref, ref, self.ag_s.at[0], recv, self.sib).wait_recv()
 
-    def ag(self, bank):
+    def ag(self, bank, start, latest=1e9):
         A = self.A
-        info, steps = self.orders(self.ag_parts), []
+        info = self.orders(self.ag_parts)
 
         def z_sends(part, f, fc, lc, w):
             px, py = self.place(f, fc, lc)
@@ -232,16 +244,22 @@
 
         bigs = [row for row in info if row[1]]
         smalls = [row for row in info if not row[1]]
-        steps += [early, begin]
+        due = [(start - EARLY, early), (start, begin)]
         for d in range(1, A):
-            steps += [functools.partial(arrive, d, 0, *row) for row in info]
-            if d == 1:
-                steps += [functools.partial(beside, *row) for row in bigs]
-            steps += [functools.partial(arrive, d, 1, *row) for row in bigs]
-            steps += [functools.partial(cross, d - 1, *row) for row in smalls]
-        steps += [functools.partial(cross, A - 1, *row) for row in smalls]
-        steps += [functools.partial(self.ag_last, bank, row[0]) for row in info]
-        return steps
+            for k, row in enumerate(info):
+                come = start + COME + PLANE * (d - 1) + STEP * k
+                due.append((come, functools.partial(arrive, d, 0, *row)))
+                if row[1]:
+                    side = start + BESIDE + STEP * k
+                    if d == 1:
+                        due.append((side, functools.partial(beside, *row)))
+                    due.append((max(come + STEP * len(info), side + 0.1), functools.partial(arrive, d, 1, *row)))
+                else:
+                    if d == 1:
+                        due.append((start + CROSS + STEP * k, functools.partial(cross, 0, *row)))
+                    over = start + CROSS + PLANE * d + STEP * k
+                    due.append((max(over, come + 0.1), functools.partial(cross, d, *row)))
+        return [(min(time, latest), step) for time, step in due]
 
     def planes_at(self, d, act):
         if d == 0:
@@ -736,6 +754,7 @@
     s = Layer(A, R, T, ag_parts, rs_parts, dict(zip(names, arrays)))
     s.land = [getattr(s, f"land{i}") for i in range(len(rs_parts))]
     D = s.D
+    s.n2r, s.ga = s.nga.at[0], s.nga.at[1]
     away = jnp.logical_not(s.kept)
     s.ng[...] = jnp.zeros_like(s.ng)
     s.pfx_own[...] = jnp.full(s.pfx_own.shape, s.pfx[0], jnp.int32).astype(F32)
@@ -791,9 +810,6 @@
         def _():
             s.remote(src, far, s.sw_s.at[i], s.sw_r.at[i], s.partner).start()
 
-    swap(0)
-    swap(1)
-    swap(2)
 
     @pl.when(by_rows)
     def _():
@@ -806,8 +822,14 @@
         half_send.wait_send()
         half_recv.wait_recv()
 
-    gather, ffn = Steps(s.ag(0)), Steps(s.ag(1))
-    gather.run(2)
+    def both():
+        for copy in ffn_copies:
+            copy.wait()
+
+    due = s.ag(0, EARLY, GATHERED) + s.ag(1, SECOND_BANK) + [(SECOND_BANK - EARLY - 0.1, both)]
+    due += [(SWAPS, functools.partial(swap, i)) for i in range(3)] + [(LATE_SWAP, functools.partial(swap, 3))]
+    gather = Steps(sorted(due, key=lambda step: step[0]))
+    gather.until(EARLY)
 
     def swapped(i):
         src, dst, far = swaps[i]
@@ -821,35 +843,33 @@
             s.remote(src, far, s.sw_s.at[i], s.sw_r.at[i], s.partner).wait_send()
             s.remote(src, dst, s.sw_s.at[i], s.sw_r.at[i], s.partner).wait_recv()
 
-    gather.run(14)
-    for copy in ffn_copies:
-        copy.wait()
-    ffn.run(1)
-    gather.run(14)
-    ffn.run(1)
-    swap(3)
+    gather.until(GATHERED)
     for i in range(3):
         swapped(i)
     s.share(s.xf, 0)
     s.share(s.mf, 1)
-    gather.finish()
+    for part in range(len(ag_parts)):
+        s.ag_last(0, part)
     s.shared(s.xf, 0)
     s.shared(s.mf, 1)
 
+    def clock(time):
+        return GATHERED + RATE * time
+
     s.project(s.qkv1, 0, s.xf, 0, 3)
-    ffn.run(2)
+    gather.until(clock(2.0))
     s.project(s.qkv2, 1, s.mf, 5, 2)
-    ffn.run(2)
+    gather.until(clock(3.5))
 
     @pl.loop(0, TILE // PAIR)
     def _(p):
-        s.attend(p, s.qkv1, s.o1, s.lse1, True, ffn.spread(p, TILE // PAIR, 4))
+        s.attend(p, s.qkv1, s.o1, s.lse1, True, gather.timed(p, TILE // PAIR, 4, clock(3.5), RATE * 8.0))
 
     def branch(o, b):
         return lambda which: [dot(o[s.rows_of(which), :], s.wrow(b, h)) for h in range(2)]
 
     s.give(0, branch(s.o1, 3))
-    ffn.run(1)
+    gather.until(clock(13.5))
     s.taken(0)
 
     def first_norm(own, full):
@@ -863,17 +883,17 @@
 
     s.norm_rows(first_norm)
     s.share(s.n1r, 2)
-    ffn.run(2)
+    gather.until(clock(16.0))
     s.shared(s.n1r, 2)
 
     s.project(s.qkv2, 0, s.n1r, 4, 1)
 
     @pl.loop(0, TILE // PAIR)
     def _(p):
-        s.attend(p, s.qkv2, s.o2, s.lse2, False, ffn.spread(p, TILE // PAIR, 4))
+        s.attend(p, s.qkv2, s.o2, s.lse2, False, gather.timed(p, TILE // PAIR, 4, clock(17.0), RATE * 8.0))
 
     s.give(1, branch(s.o2, 7))
-    ffn.run(1)
+    gather.until(clock(27.0))
     s.taken(1)
 
     def second_norm(own, full):
@@ -887,9 +907,11 @@
 
     s.norm_rows(second_norm)
     s.share(s.n2r, 3)
-    ffn.run(2)
+    gather.until(clock(29.5))
     s.shared(s.n2r, 3)
-    ffn.finish()
+    gather.until(1e9)
+    for part in range(len(ag_parts)):
+        s.ag_last(1, part)
     swapped(3)
 
     tiles = 2 * A * R // TILE
@@ -943,19 +965,30 @@
 
     s.give(3, ffn_in)
 
-    @pl.loop(0, tiles)
-    def _(j):
-        hidden, grads = s.act_all(tiles + j), s.act_all(j)
+    def hidden_terms(tile):
+        hidden = s.act_all(tile)
         for h in range(2):
-            cols = slice(h * TILE, (h + 1) * TILE)
-            out_rows = dot_tn(hidden, s.ga[:, cols]).astype(BF)
-            s.wb[pl.ds(3 * A + j * s.nt, s.nt), h] = out_rows.reshape(s.nt, 2 * R, TILE)
-            in_rows = dot_tn(grads, s.n2r[:, cols]).astype(BF)
-            s.wb[pl.ds(2 * A + j * s.nt, s.nt), h] = in_rows.reshape(s.nt, 2 * R, TILE)
+            terms = dot_tn(hidden, s.nga[tile // tiles, :, h * TILE : (h + 1) * TILE]).astype(BF)
+            s.wb[pl.ds(2 * A + tile * s.nt, s.nt), h] = terms.reshape(s.nt, 2 * R, TILE)
+
+    spread = Steps(s.rs(s.dffn, s.fin), ACROSS * A)
+    if s.nt == 1:
+        for x in range(2):
+            hidden_terms(2 * s.turns[0] + x)
+        spread.until(0.0)
+
+        @pl.loop(2, 2 * A)
+        def _(k):
+            hidden_terms(2 * s.turn(k // 2) + lax.rem(k, 2))
+    else:
+
+        @pl.loop(0, 2 * tiles)
+        def _(k):
+            hidden_terms(k)
+
+        spread.until(0.0)
 
     s.f_credit(None, 0)
-    spread = Steps(s.rs(s.dffn, s.fin), ACROSS * A)
-    spread.until(0.0)
     s.taken(3)
 
     def second_back(own, full):
@@ -1100,7 +1133,8 @@
     spread.until(1e9)
     s.f_credit(pl.semaphore_wait, 0)
     spread.limit = 1e9
-    spread.until(ACROSS * A + 4.0)
+
+    spread.until(MIDDLE)
 
     @pl.when(away)
     def _():
@@ -1185,8 +1219,7 @@
         xf=low(2 * T, D),
         mf=low(2 * T, D),
         n1r=low(2 * T, D),
-        n2r=low(2 * T, D),
-        ga=low(2 * T, D),
+        nga=low(2, 2 * T, D),
         gb=low(2 * T, D),
         cotb=low(T, D),
         act=low(2 * A, 2, R, TILE),

time: 328 us -> 309 us (0.942)
  the two profiles are of different devices: /device:TPU:19 before, /device:TPU:9 now
where the time goes in v4:
time: 309 us; the launch traced here: 303 us
  Pallas kernels  302 us (98%)
    pallas_call x1, Pallas kernels, on_device(): pl.pallas_call(functools.partial(kernel, A, R, T, ag_parts, rs_parts, nam...  296 us

profile of v4, /device:TPU:9, one launch (start us, length us, event | category | flops | bytes accessed | tf_op | source)
XLA Modules:
  0.0 303.4 jit_solution(13469416663462068679)
XLA Ops:
  1.3 296.3 %layer.1 = (f32[256,1024]{1,0:T(8,128)}, f32[256,1024]{1,0:T(8,128)}, f32[256,1024]{1,0:T(8,128)}, f32[256,1024]{1,0:T(8,128)}, f32[256,1024]{1,0:T(8,128)}, /*index=5*/f32[6,1024]{1,0:T(8,128)}) custom-call(bf16[256,1024]{1,0:T(8,128)(2,1)} %arrays_0_.1, bf16[256,1024]{1,0:T(8,128)(2,1)} %arrays_1_.1, bf16[256,1024]{1,0:T(8,128)(2,1)} %arrays_2_.1, ...), custom_call_target="tpu_custom_call" | custom-call | tf_op jit(solution)/shard_map/layer/pallas_call | solution.py:1271
  297.6 5.3 %hand_on.1 = (f32[256,1024]{1,0:T(8,128)}, f32[256,1024]{1,0:T(8,128)}, f32[256,1024]{1,0:T(8,128)}, f32[256,1024]{1,0:T(8,128)}, f32[256,1024]{1,0:T(8,128)}, /*index=5*/f32[6,1024]{1,0:T(8,128)}) custom-call(f32[256,1024]{1,0:T(8,128)} %get-tuple-element.12.refs_0_, f32[256,1024]{1,0:T(8,128)} %get-tuple-element.13.refs_1_, ...), custom_call_target="tpu_custom_call" | custom-call | tf_op jit(solution)/shard_map/hand_on/pallas_call | solution.py:1283
